TPU v7x, 256 devices: a whole 4x4x8 slice. The times are simulated.
256 devices in a mesh: ctx: 64 (over x_lo, y, z), head: 4 (over x_hi, core).
Axes of the slice: x: 4 (x_hi: 2, x_lo: 2; x = x_hi * 2 + x_lo), y: 4, z: 8, core: 2. Of those that a mesh axis runs over, the one named last changes fastest.
Arguments:
- queries: bfloat16 [64, 3, 256, 2048], P('ctx', None, None, 'head'), may hold values from -5 to 5
- keys: bfloat16 [64, 3, 256, 2048], P('ctx', None, None, 'head'), may hold values from -5 to 5
- values: bfloat16 [64, 3, 256, 2048], P('ctx', None, None, 'head'), may hold values from -6 to 6
- grad_out: bfloat16 [64, 3, 256, 2048], P('ctx', None, 'head'), may hold values from -6 to 6
- window_start: int32 [64, 3], replicated, may hold values from 0 to 61, as said below
- key_counts: int32 [64, 3], replicated, may hold values from 64 to 256, as said below
Outputs:
- attended: bfloat16 [64, 3, 256, 2048], P('ctx', None, None, 'head')
- grad_queries: bfloat16 [64, 3, 256, 2048], P('ctx', None, None, 'head')
- grad_keys: bfloat16 [64, 3, 256, 2048], P('ctx', None, None, 'head')
- grad_values: bfloat16 [64, 3, 256, 2048], P('ctx', None, None, 'head')
Inputs may be any that keep to these rules, and one draw needn't show every extreme that they name: window_start[c, t] = clip(c - r, 0, 61) with r one of 0 to 2. `key_counts`: only tiles of the last of the 3 time tiles hold fewer than 256 live tokens.
All inputs are finite; a program needn't handle non-finite values.
Results may differ from a plain program's by a relative error of at most 0.011.
Values may be sent and summed in bfloat16 or wider, within the bound.
A program may use at most 128 MiB of HBM per device.

v0:
```python
import jax
import jax.numpy as jnp
from jax import lax
from jax.sharding import PartitionSpec as P

DH = 128
WIN = 3


def from_behind(value, axis, steps):
    count = lax.axis_size(axis)
    first, last = (max(0, -steps), min(count, count - steps))
    return lax.ppermute(value, axis, [(source, source + steps) for source in range(first, last)])


def to_heads(block):
    columns, tile_len, width = block.shape
    return block.reshape(columns, tile_len, width // DH, DH).transpose(2, 0, 1, 3)


def from_heads(block):
    head_count, columns, tile_len, features = block.shape
    return block.transpose(1, 2, 0, 3).reshape(columns, tile_len, head_count * features)


def local_tile(query, grad, key_block, value_block, live):
    factor = DH ** (-0.5)
    scores = (
        jnp.einsum("hqd,hkd->hqk", query, key_block, preferred_element_type=jnp.float32) * factor
    )
    scores = jnp.where(live[None, None, :], scores, -jnp.inf)
    row_max = jnp.max(scores, axis=-1, keepdims=True)
    total = jnp.sum(jnp.exp(scores - row_max), axis=-1, keepdims=True)
    log_total = row_max + jnp.log(total)
    probs = jnp.exp(scores - log_total)
    weights = probs.astype(jnp.bfloat16)
    attended = jnp.einsum(
        "hqk,hkd->hqd", weights, value_block, preferred_element_type=jnp.float32
    ).astype(jnp.bfloat16)
    delta = jnp.sum(grad.astype(jnp.float32) * attended.astype(jnp.float32), axis=-1)
    dprobs = jnp.einsum("hqd,hkd->hqk", grad, value_block, preferred_element_type=jnp.float32)
    dscores = (probs * (dprobs - delta[:, :, None])).astype(jnp.bfloat16)
    grad_query = (
        jnp.einsum("hqk,hkd->hqd", dscores, key_block, preferred_element_type=jnp.float32) * factor
    ).astype(jnp.bfloat16)
    return (attended, grad_query, weights, dscores, log_total[:, :, 0], delta)


def key_terms(weights, dscores, query, grad):
    factor = DH ** (-0.5)
    key_part = (
        jnp.einsum("hqk,hqd->hkd", dscores, query, preferred_element_type=jnp.float32) * factor
    )
    value_part = jnp.einsum("hqk,hqd->hkd", weights, grad, preferred_element_type=jnp.float32)
    return jnp.stack([key_part, value_part])


def shift_keys(local_pair):
    slabs = []
    for offset in range(1 - WIN, WIN):
        if offset == 0:
            slabs.append(local_pair)
        else:
            slabs.append(from_behind(local_pair, "ctx", -offset))
    return jnp.stack(slabs, axis=2)


def shards(queries, keys, values, grad_out, window_start, key_counts):
    position = lax.axis_index("ctx")
    columns = queries.shape[1]
    tile_len = queries.shape[2]
    width = queries.shape[3]
    head_count = width // DH
    breadth = min(WIN, columns)
    window_keys = WIN * breadth * tile_len
    positions = jnp.arange(tile_len, dtype=jnp.int32)
    zero = jnp.zeros((), jnp.int32)
    grad_here = lax.all_to_all(grad_out, "head", split_axis=3, concat_axis=2, tiled=True)
    queries_heads = to_heads(queries[0])
    grad_heads = to_heads(grad_here[0])
    local_pair = jnp.stack([to_heads(keys[0]), to_heads(values[0])])
    neighbours = shift_keys(local_pair)
    partial_value = jnp.zeros((2, head_count, 2 * WIN - 1, columns, tile_len, DH), jnp.float32)
    attended_all = jnp.zeros((head_count, columns, tile_len, DH), jnp.bfloat16)
    grad_query_all = jnp.zeros((head_count, columns, tile_len, DH), jnp.bfloat16)
    stats_all = jnp.zeros((2, head_count, columns, tile_len), jnp.float32)

    def visit(column, carry):
        attended_all, grad_query_all, stats_all, partial_value = carry
        first_time = window_start[position, column]
        first_col = jnp.clip(column - 1, 0, columns - breadth).astype(jnp.int32)
        relative = first_time - position + WIN - 1
        block = lax.dynamic_slice(
            neighbours,
            (zero, zero, relative, first_col, zero, zero),
            (2, head_count, WIN, breadth, tile_len, DH),
        )
        block = block.reshape(2, head_count, window_keys, DH)
        counts = lax.dynamic_slice(key_counts, (first_time, first_col), (WIN, breadth))
        live = (positions[None, None, :] < counts[:, :, None]).reshape(window_keys)
        query = lax.dynamic_index_in_dim(queries_heads, column, 1, False)
        grad = lax.dynamic_index_in_dim(grad_heads, column, 1, False)
        attended, grad_query, weights, dscores, log_total, delta = local_tile(
            query, grad, block[0], block[1], live
        )
        attended_all = lax.dynamic_update_index_in_dim(attended_all, attended, column, 1)
        grad_query_all = lax.dynamic_update_index_in_dim(grad_query_all, grad_query, column, 1)
        terms = key_terms(weights, dscores, query, grad).reshape(
            2, head_count, WIN, breadth, tile_len, DH
        )
        start = (zero, zero, relative, first_col, zero, zero)
        partial_value = lax.dynamic_update_slice(
            partial_value, lax.dynamic_slice(partial_value, start, terms.shape) + terms, start
        )
        return (attended_all, grad_query_all, stats_all, partial_value)

    attended_all, grad_query_all, stats_all, partial_value = lax.fori_loop(
        0, columns, visit, (attended_all, grad_query_all, stats_all, partial_value)
    )
    own_terms = partial_value[:, :, WIN - 1]
    for offset in range(1 - WIN, WIN):
        if offset != 0:
            own_terms = own_terms + from_behind(
                partial_value[:, :, offset + WIN - 1].astype(jnp.bfloat16), "ctx", offset
            ).astype(jnp.float32)
    grad_keys = from_heads(own_terms[0].astype(jnp.bfloat16))[None]
    grad_values = from_heads(own_terms[1].astype(jnp.bfloat16))[None]
    return (
        from_heads(attended_all)[None],
        from_heads(grad_query_all)[None],
        grad_keys,
        grad_values,
    )


def solution(mesh):
    placed = (
        P("ctx", None, None, "head"),
        P("ctx", None, None, "head"),
        P("ctx", None, None, "head"),
        P("ctx", None, "head", None),
        P(),
        P(),
    )
    return jax.shard_map(
        shards,
        mesh=mesh,
        in_specs=placed,
        out_specs=(
            P("ctx", None, None, "head"),
            P("ctx", None, None, "head"),
            P("ctx", None, None, "head"),
            P("ctx", None, None, "head"),
        ),
        check_vma=False,
    )
```

profile of v0, /device:TPU:25, one launch (start us, length us, event | category | flops | bytes accessed | tf_op | source)
XLA Modules:
  0.0 408.4 jit_solution(4311587588089583702)
XLA Ops:
  5.3 4.9 %collective-permute-start = (bf16[2,4,3,256,128]{3,4,1,2,0:T(8,128)(2,1)}, bf16[2,4,3,256,128]{3,4,1,2,0:T(8,128)(2,1)}, u32[]{:S(2)}, u32[]{:S(2)}) collective-permute-start(bf16[2,4,3,256,128]{3,4,1,2,0:T(8,128)(2,1)} %pad_maximum_fusion), channel_id=1, source_target_pairs={{0,8},{4,12},{8,16},{12,20},{16,24},{20,28},{24,32},{28,36},{32,40... | collective-permute-start | bytes 4718600 | tf_op jit(solution)/shard_map/ppermute | solution.py:13
  10.2 3.5 collective-permute-start.1
  13.7 3.8 collective-permute-start.2
  21.5 5.8 %all-to-all-start = ((bf16[4,2,49152]{2,1,0:T(2,128)(2,1)}), bf16[4,2,49152]{2,1,0:T(2,128)(2,1)}, u32[]{:S(2)}, u32[]{:S(2)}) async-start(bf16[4,2,49152]{2,1,0:T(2,128)(2,1)} %reshape.96), calls=%async_computation | async-start | bytes 1572864 | tf_op jit(solution)/shard_map/all_to_all | solution.py:78
  31.9 28.2 %all-to-all-done = bf16[4,2,49152]{2,1,0:T(2,128)(2,1)} async-done(((bf16[4,2,49152]{2,1,0:T(2,128)(2,1)}), bf16[4,2,49152]{2,1,0:T(2,128)(2,1)}, u32[]{:S(2)}, u32[]{:S(2)}) %all-to-all-start) | async-done | bytes 786464 | tf_op jit(solution)/shard_map/all_to_all | solution.py:78
  69.8 45.2 %collective-permute-done.1 = bf16[2,4,3,256,128]{3,4,1,2,0:T(8,128)(2,1)} collective-permute-done((bf16[2,4,3,256,128]{3,4,1,2,0:T(8,128)(2,1)}, bf16[2,4,3,256,128]{3,4,1,2,0:T(8,128)(2,1)}, u32[]{:S(2)}, u32[]{:S(2)}) %collective-permute-start.1) | collective-permute-done | bytes 1572896 | tf_op jit(solution)/shard_map/ppermute | solution.py:13
  124.5 7.5 %broadcast_in_dim.84 = f32[2,4,5,3,256,128]{5,4,3,2,1,0:T(8,128)} broadcast(f32[]{:T(128)} %constant.153.clone.1), dimensions={} | broadcast | bytes 15728644 | tf_op jit(solution)/shard_map/broadcast_in_dim | solution.py:83
  132.0 150.8 %while.22 = (s32[]{:T(128)}, bf16[4,3,256,128]{2,3,0,1:T(8,128)(2,1)}, bf16[4,3,256,128]{3,2,0,1:T(8,128)(2,1)}, f32[2,4,5,3,256,128]{5,4,3,2,1,0:T(8,128)}, s32...) while((s32[]{:T(128)}, ...), condition=%wide.region_4.5_spmd.clone, body=%wide.region_0.4_spmd.clone.sunk | while | flops 3661365504 | bytes 152885616 | solution.py:117
  136.4 5.2 %constant_dynamic-slice_fusion.7 = (bf16[1,4,3,3,256,128]{4,5,1,3,0,2:T(8,128)(2,1)}, bf16[1,4,3,3,256,128]{4,5,1,3,0,2:T(8,128)(2,1)}) fusion(bf16[2,4,5,3,256,128]{4,5,1,3,0,2:T(8,128)(2,1)} %get-tuple-element.581, s32[]{:T(128)S(6)} %select_n.79, s32[]{:T(128)S(6)} %add.197), kind=kLoop, calls=%fused_computation.27.clone.1 | loop fusion | bytes 9437192 | tf_op jit(solution)/shard_map/while/body/eval_jaxpr/slice | solution.py:104
  144.6 4.3 %copy.87 = bf16[1,4,3,3,256,128]{5,4,3,2,1,0:T(8,128)(2,1)} copy(bf16[1,4,3,3,256,128]{4,5,1,3,0,2:T(8,128)(2,1)} %get-tuple-element.533) | data formatting | bytes 4718592 | tf_op jit(solution)/shard_map/while
  148.9 3.4 fusion.58
  159.5 4.6 %fusion.60 = f32[4,2304,128]{2,1,0:T(8,128)} fusion(f32[4,256,2304]{2,1,0:T(8,128)S(1)} %get-tuple-element.534, f32[4,256]{1,0:T(4,128)S(1)} %log_add_fusion.2, bf16[4,1,256,128]{2,3,0,1:T(8,128)(2,1)S(1)} %copy.89), kind=kOutput, calls=%fused_computation.9.clone.1 | convolution fusion | flops 608698368 | bytes 14422016 | tf_op jit(solution)/shard_map/while/body/eval_jaxpr/hqk,hqd->hkd/dot_general | solution.py:54
  165.7 4.0 convolution_multiply_fusion.3
  169.7 12.5 %fusion.61 = f32[2,4,5,3,256,128]{5,4,3,2,1,0:T(8,128)} fusion(f32[2,4,5,3,256,128]{5,4,3,2,1,0:T(8,128)} %get-tuple-element.558, s32[]{:T(128)S(6)} %select_n.79, f32[1,4,3,3,256,128]{5,4,3,2,1,0:T(8,128)} %bitcast.130, f32[1,4,3,3,256,128]{5,4,3,2,1,0:T(8,128)} %bitcast.131), kind=kLoop, calls=%fused_computation.2.clone.1 | loop fusion | flops 4718592 | bytes 28311556 | tf_op jit(solution)/shard_map/while/body/eval_jaxpr/dynamic_update_slice | solution.py:112
  186.6 5.2 %constant_dynamic-slice_fusion.7 = (bf16[1,4,3,3,256,128]{4,5,1,3,0,2:T(8,128)(2,1)}, bf16[1,4,3,3,256,128]{4,5,1,3,0,2:T(8,128)(2,1)}) fusion(bf16[2,4,5,3,256,128]{4,5,1,3,0,2:T(8,128)(2,1)} %get-tuple-element.581, s32[]{:T(128)S(6)} %select_n.79, s32[]{:T(128)S(6)} %add.197), kind=kLoop, calls=%fused_computation.27.clone.1 | loop fusion | bytes 9437192 | tf_op jit(solution)/shard_map/while/body/eval_jaxpr/slice | solution.py:104
  194.9 4.3 %copy.87 = bf16[1,4,3,3,256,128]{5,4,3,2,1,0:T(8,128)(2,1)} copy(bf16[1,4,3,3,256,128]{4,5,1,3,0,2:T(8,128)(2,1)} %get-tuple-element.533) | data formatting | bytes 4718592 | tf_op jit(solution)/shard_map/while
  199.1 3.4 fusion.58
  209.8 4.6 %fusion.60 = f32[4,2304,128]{2,1,0:T(8,128)} fusion(f32[4,256,2304]{2,1,0:T(8,128)S(1)} %get-tuple-element.534, f32[4,256]{1,0:T(4,128)S(1)} %log_add_fusion.2, bf16[4,1,256,128]{2,3,0,1:T(8,128)(2,1)S(1)} %copy.89), kind=kOutput, calls=%fused_computation.9.clone.1 | convolution fusion | flops 608698368 | bytes 14422016 | tf_op jit(solution)/shard_map/while/body/eval_jaxpr/hqk,hqd->hkd/dot_general | solution.py:54
  215.9 4.0 convolution_multiply_fusion.3
  219.9 12.6 %fusion.61 = f32[2,4,5,3,256,128]{5,4,3,2,1,0:T(8,128)} fusion(f32[2,4,5,3,256,128]{5,4,3,2,1,0:T(8,128)} %get-tuple-element.558, s32[]{:T(128)S(6)} %select_n.79, f32[1,4,3,3,256,128]{5,4,3,2,1,0:T(8,128)} %bitcast.130, f32[1,4,3,3,256,128]{5,4,3,2,1,0:T(8,128)} %bitcast.131), kind=kLoop, calls=%fused_computation.2.clone.1 | loop fusion | flops 4718592 | bytes 28311556 | tf_op jit(solution)/shard_map/while/body/eval_jaxpr/dynamic_update_slice | solution.py:112
  236.9 5.2 %constant_dynamic-slice_fusion.7 = (bf16[1,4,3,3,256,128]{4,5,1,3,0,2:T(8,128)(2,1)}, bf16[1,4,3,3,256,128]{4,5,1,3,0,2:T(8,128)(2,1)}) fusion(bf16[2,4,5,3,256,128]{4,5,1,3,0,2:T(8,128)(2,1)} %get-tuple-element.581, s32[]{:T(128)S(6)} %select_n.79, s32[]{:T(128)S(6)} %add.197), kind=kLoop, calls=%fused_computation.27.clone.1 | loop fusion | bytes 9437192 | tf_op jit(solution)/shard_map/while/body/eval_jaxpr/slice | solution.py:104
  245.1 4.3 %copy.87 = bf16[1,4,3,3,256,128]{5,4,3,2,1,0:T(8,128)(2,1)} copy(bf16[1,4,3,3,256,128]{4,5,1,3,0,2:T(8,128)(2,1)} %get-tuple-element.533) | data formatting | bytes 4718592 | tf_op jit(solution)/shard_map/while
  249.4 3.4 fusion.58
  260.0 4.6 %fusion.60 = f32[4,2304,128]{2,1,0:T(8,128)} fusion(f32[4,256,2304]{2,1,0:T(8,128)S(1)} %get-tuple-element.534, f32[4,256]{1,0:T(4,128)S(1)} %log_add_fusion.2, bf16[4,1,256,128]{2,3,0,1:T(8,128)(2,1)S(1)} %copy.89), kind=kOutput, calls=%fused_computation.9.clone.1 | convolution fusion | flops 608698368 | bytes 14422016 | tf_op jit(solution)/shard_map/while/body/eval_jaxpr/hqk,hqd->hkd/dot_general | solution.py:54
  266.2 4.0 convolution_multiply_fusion.3
  270.2 12.5 %fusion.61 = f32[2,4,5,3,256,128]{5,4,3,2,1,0:T(8,128)} fusion(f32[2,4,5,3,256,128]{5,4,3,2,1,0:T(8,128)} %get-tuple-element.558, s32[]{:T(128)S(6)} %select_n.79, f32[1,4,3,3,256,128]{5,4,3,2,1,0:T(8,128)} %bitcast.130, f32[1,4,3,3,256,128]{5,4,3,2,1,0:T(8,128)} %bitcast.131), kind=kLoop, calls=%fused_computation.2.clone.1 | loop fusion | flops 4718592 | bytes 28311556 | tf_op jit(solution)/shard_map/while/body/eval_jaxpr/dynamic_update_slice | solution.py:112
  282.8 7.3 %slice_bitcast_fusion.3 = (bf16[2,4,3,256,128]{4,3,2,1,0:T(8,128)(2,1)}, bf16[2,4,3,256,128]{4,3,2,1,0:T(8,128)(2,1)}, bf16[2,4,3,256,128]{4,3,2,1,0:T(8,128)(2,1)}, bf16[2,4,3,256,128]{4,3,2,1,0:T(8,128)(2,1)S(1)}) fusion(f32[2,4,5,3,256,128]{5,4,3,2,1,0:T(8,128)} %get-tuple-element.367), kind=kLoop, calls=%fused_computation.41 | loop fusion | bytes 12582912 | tf_op jit(solution)/shard_map/convert_element_type | solution.py:124
  290.0 4.3 %collective-permute-start.4 = (bf16[2,4,3,256,128]{4,3,2,1,0:T(8,128)(2,1)}, bf16[2,4,3,256,128]{4,3,2,1,0:T(8,128)(2,1)}, u32[]{:S(2)}, u32[]{:S(2)}) collective-permute-start(bf16[2,4,3,256,128]{4,3,2,1,0:T(8,128)(2,1)} %get-tuple-element.453), channel_id=1, source_target_pairs={{8,0},{12,4},{16,8},{20,12},{24,16},{28,20},{32,24},{36,28},{40,32... | collective-permute-start | bytes 4718600 | tf_op jit(solution)/shard_map/ppermute | solution.py:13
  298.6 5.0 %collective-permute-start.5 = (bf16[2,4,3,256,128]{4,3,2,1,0:T(8,128)(2,1)S(1)}, bf16[2,4,3,256,128]{4,3,2,1,0:T(8,128)(2,1)}, u32[]{:S(2)}, u32[]{:S(2)}) collective-permute-start(bf16[2,4,3,256,128]{4,3,2,1,0:T(8,128)(2,1)S(1)} %get-tuple-element.456), channel_id=1, source_target_pairs={{4,0},{8,4},{12,8},{16,12},{20,16},{24,20},{28,24},{32,28},{36,32}... | collective-permute-start | bytes 4718600 | tf_op jit(solution)/shard_map/ppermute | solution.py:13
  306.6 56.2 %collective-permute-done.4 = bf16[2,4,3,256,128]{4,3,2,1,0:T(8,128)(2,1)} collective-permute-done((bf16[2,4,3,256,128]{4,3,2,1,0:T(8,128)(2,1)}, bf16[2,4,3,256,128]{4,3,2,1,0:T(8,128)(2,1)}, u32[]{:S(2)}, u32[]{:S(2)}) %collective-permute-start.4) | collective-permute-done | bytes 1572896 | tf_op jit(solution)/shard_map/ppermute | solution.py:13
  362.8 37.0 %collective-permute-done.6 = bf16[2,4,3,256,128]{4,3,2,1,0:T(8,128)(2,1)} collective-permute-done((bf16[2,4,3,256,128]{4,3,2,1,0:T(8,128)(2,1)}, bf16[2,4,3,256,128]{4,3,2,1,0:T(8,128)(2,1)}, u32[]{:S(2)}, u32[]{:S(2)}) %collective-permute-start.6) | collective-permute-done | bytes 1572896 | tf_op jit(solution)/shard_map/ppermute | solution.py:13
  399.8 4.9 %fusion.25 = bf16[2,4,3,256,128]{4,3,2,1,0:T(8,128)(2,1)S(1)} fusion(bf16[2,4,3,256,128]{4,3,2,1,0:T(8,128)(2,1)} %collective-permute-done.7, bf16[2,4,3,256,128]{4,3,2,1,0:T(8,128)(2,1)} %collective-permute-done.6, bf16[2,4,3,256,128]{4,3,2,1,0:T(8,128)(2,1)} %collective-permute-done.5, bf16[2,4,3,256,128]{4,3,2,1,0:T(8,128)(2,1)} %collective-permute-done.4, ...), kind=kLoop, calls=%fused_computation.37 | loop fusion | flops 7077888 | bytes 11010048 | tf_op jit(solution)/shard_map/convert.1
  (120 shorter events, 83.8 us)
Async XLA Ops:
  0.6 17.0 %copy-start.11 = (bf16[1,3,64,2048]{3,2,1,0:T(8,128)(2,1)S(1)}, bf16[1,3,64,2048]{3,2,1,0:T(8,128)(2,1)}, u32[]{:S(2)}) copy-start(bf16[1,3,64,2048]{3,2,1,0:T(8,128)(2,1)} %param.11) | copy-start | bytes 2359300
  2.1 11.6 %copy-start.1 = (bf16[1,3,256,512]{2,3,1,0:T(8,128)(2,1)}, bf16[1,3,256,512]{2,3,1,0:T(8,128)(2,1)S(1)}, u32[]{:S(2)}) copy-start(bf16[1,3,256,512]{2,3,1,0:T(8,128)(2,1)S(1)} %copy.54) | copy-start | bytes 2359300
  3.8 9.9 %copy-start.3 = (bf16[1,3,256,512]{2,3,1,0:T(8,128)(2,1)}, bf16[1,3,256,512]{2,3,1,0:T(8,128)(2,1)S(1)}, u32[]{:S(2)}) copy-start(bf16[1,3,256,512]{2,3,1,0:T(8,128)(2,1)S(1)} %copy.55) | copy-start | bytes 2359300
  5.3 61.9 %collective-permute-start = (bf16[2,4,3,256,128]{3,4,1,2,0:T(8,128)(2,1)}, bf16[2,4,3,256,128]{3,4,1,2,0:T(8,128)(2,1)}, u32[]{:S(2)}, u32[]{:S(2)}) collective-permute-start(bf16[2,4,3,256,128]{3,4,1,2,0:T(8,128)(2,1)} %pad_maximum_fusion), channel_id=1, source_target_pairs={{0,8},{4,12},{8,16},{12,20},{16,24},{20,28},{24,32},{28,36},{32,40... | collective-permute-start | bytes 4718600 | tf_op jit(solution)/shard_map/ppermute | solution.py:13
  10.2 104.9 %collective-permute-start.1 = (bf16[2,4,3,256,128]{3,4,1,2,0:T(8,128)(2,1)}, bf16[2,4,3,256,128]{3,4,1,2,0:T(8,128)(2,1)}, u32[]{:S(2)}, u32[]{:S(2)}) collective-permute-start(bf16[2,4,3,256,128]{3,4,1,2,0:T(8,128)(2,1)} %pad_maximum_fusion), channel_id=1, source_target_pairs={{0,4},{4,8},{8,12},{12,16},{16,20},{20,24},{24,28},{28,32},{32,36}... | collective-permute-start | bytes 4718600 | tf_op jit(solution)/shard_map/ppermute | solution.py:13
  13.7 105.3 %collective-permute-start.2 = (bf16[2,4,3,256,128]{3,4,1,2,0:T(8,128)(2,1)}, bf16[2,4,3,256,128]{3,4,1,2,0:T(8,128)(2,1)}, u32[]{:S(2)}, u32[]{:S(2)}) collective-permute-start(bf16[2,4,3,256,128]{3,4,1,2,0:T(8,128)(2,1)} %pad_maximum_fusion), channel_id=1, source_target_pairs={{4,0},{8,4},{12,8},{16,12},{20,16},{24,20},{28,24},{32,28},{36,32}... | collective-permute-start | bytes 4718600 | tf_op jit(solution)/shard_map/ppermute | solution.py:13
  21.5 38.6 %all-to-all-start = ((bf16[4,2,49152]{2,1,0:T(2,128)(2,1)}), bf16[4,2,49152]{2,1,0:T(2,128)(2,1)}, u32[]{:S(2)}, u32[]{:S(2)}) async-start(bf16[4,2,49152]{2,1,0:T(2,128)(2,1)} %reshape.96), calls=%async_computation | async-start | bytes 1572864 | tf_op jit(solution)/shard_map/all_to_all | solution.py:78
  27.3 94.5 %collective-permute-start.3 = (bf16[2,4,3,256,128]{3,4,1,2,0:T(8,128)(2,1)}, bf16[2,4,3,256,128]{3,4,1,2,0:T(8,128)(2,1)}, u32[]{:S(2)}, u32[]{:S(2)}) collective-permute-start(bf16[2,4,3,256,128]{3,4,1,2,0:T(8,128)(2,1)} %pad_maximum_fusion), channel_id=1, source_target_pairs={{8,0},{12,4},{16,8},{20,12},{24,16},{28,20},{32,24},{36,28},{40,32... | collective-permute-start | bytes 4718600 | tf_op jit(solution)/shard_map/ppermute | solution.py:13
  65.3 52.5 %copy-start.2 = (bf16[1,3,256,512]{2,3,1,0:T(8,128)(2,1)S(1)}, bf16[1,3,256,512]{2,3,1,0:T(8,128)(2,1)}, u32[]{:S(2)}) copy-start(bf16[1,3,256,512]{2,3,1,0:T(8,128)(2,1)} %copy-done.1) | copy-start | bytes 2359300
  65.3 52.5 %copy-start.4 = (bf16[1,3,256,512]{2,3,1,0:T(8,128)(2,1)S(1)}, bf16[1,3,256,512]{2,3,1,0:T(8,128)(2,1)}, u32[]{:S(2)}) copy-start(bf16[1,3,256,512]{2,3,1,0:T(8,128)(2,1)} %copy-done.3) | copy-start | bytes 2359300
  124.5 7.5 %copy-start.12 = (s32[64,3]{0,1:T(4,128)S(1)}, s32[64,3]{0,1:T(4,128)}, u32[]{:S(2)}) copy-start(s32[64,3]{0,1:T(4,128)} %param.13) | copy-start | bytes 2308
  132.0 9.6 %copy-start.5 = (bf16[4,3,256,128]{3,0,2,1:T(4,128)(2,1)}, bf16[4,3,256,128]{3,0,2,1:T(4,128)(2,1)S(1)}, u32[]{:S(2)}) copy-start(bf16[4,3,256,128]{3,0,2,1:T(4,128)(2,1)S(1)} %get-tuple-element.582) | copy-start | bytes 2359300 | tf_op jit(solution)/shard_map/while
  159.5 4.7 %copy-start = (bf16[1,4,3,3,256,128]{5,4,3,2,1,0:T(8,128)(2,1)S(1)}, bf16[1,4,3,3,256,128]{5,4,3,2,1,0:T(8,128)(2,1)}, u32[]{:S(2)}) copy-start(bf16[1,4,3,3,256,128]{5,4,3,2,1,0:T(8,128)(2,1)} %copy.87) | copy-start | bytes 7077892 | tf_op jit(solution)/shard_map/while
  159.5 4.7 %copy-start.7 = (bf16[4,3,256,128]{3,2,0,1:T(8,128)(2,1)S(1)}, bf16[4,3,256,128]{3,2,0,1:T(8,128)(2,1)}, u32[]{:S(2)}) copy-start(bf16[4,3,256,128]{3,2,0,1:T(8,128)(2,1)} %get-tuple-element.557) | copy-start | bytes 2359300 | tf_op jit(solution)/shard_map/while
  165.7 4.0 copy-start.8
  169.7 12.6 %copy-start.6 = (bf16[4,3,256,128]{3,0,2,1:T(4,128)(2,1)S(1)}, bf16[4,3,256,128]{3,0,2,1:T(4,128)(2,1)}, u32[]{:S(2)}) copy-start(bf16[4,3,256,128]{3,0,2,1:T(4,128)(2,1)} %copy-done.5) | copy-start | bytes 2359300 | tf_op jit(solution)/shard_map/while
  182.2 9.6 %copy-start.5 = (bf16[4,3,256,128]{3,0,2,1:T(4,128)(2,1)}, bf16[4,3,256,128]{3,0,2,1:T(4,128)(2,1)S(1)}, u32[]{:S(2)}) copy-start(bf16[4,3,256,128]{3,0,2,1:T(4,128)(2,1)S(1)} %get-tuple-element.582) | copy-start | bytes 2359300 | tf_op jit(solution)/shard_map/while
  209.7 4.7 %copy-start = (bf16[1,4,3,3,256,128]{5,4,3,2,1,0:T(8,128)(2,1)S(1)}, bf16[1,4,3,3,256,128]{5,4,3,2,1,0:T(8,128)(2,1)}, u32[]{:S(2)}) copy-start(bf16[1,4,3,3,256,128]{5,4,3,2,1,0:T(8,128)(2,1)} %copy.87) | copy-start | bytes 7077892 | tf_op jit(solution)/shard_map/while
  209.8 4.7 %copy-start.7 = (bf16[4,3,256,128]{3,2,0,1:T(8,128)(2,1)S(1)}, bf16[4,3,256,128]{3,2,0,1:T(8,128)(2,1)}, u32[]{:S(2)}) copy-start(bf16[4,3,256,128]{3,2,0,1:T(8,128)(2,1)} %get-tuple-element.557) | copy-start | bytes 2359300 | tf_op jit(solution)/shard_map/while
  215.9 4.0 copy-start.8
  219.9 12.6 %copy-start.6 = (bf16[4,3,256,128]{3,0,2,1:T(4,128)(2,1)S(1)}, bf16[4,3,256,128]{3,0,2,1:T(4,128)(2,1)}, u32[]{:S(2)}) copy-start(bf16[4,3,256,128]{3,0,2,1:T(4,128)(2,1)} %copy-done.5) | copy-start | bytes 2359300 | tf_op jit(solution)/shard_map/while
  232.5 9.6 %copy-start.5 = (bf16[4,3,256,128]{3,0,2,1:T(4,128)(2,1)}, bf16[4,3,256,128]{3,0,2,1:T(4,128)(2,1)S(1)}, u32[]{:S(2)}) copy-start(bf16[4,3,256,128]{3,0,2,1:T(4,128)(2,1)S(1)} %get-tuple-element.582) | copy-start | bytes 2359300 | tf_op jit(solution)/shard_map/while
  260.0 4.7 %copy-start = (bf16[1,4,3,3,256,128]{5,4,3,2,1,0:T(8,128)(2,1)S(1)}, bf16[1,4,3,3,256,128]{5,4,3,2,1,0:T(8,128)(2,1)}, u32[]{:S(2)}) copy-start(bf16[1,4,3,3,256,128]{5,4,3,2,1,0:T(8,128)(2,1)} %copy.87) | copy-start | bytes 7077892 | tf_op jit(solution)/shard_map/while
  260.0 4.7 %copy-start.7 = (bf16[4,3,256,128]{3,2,0,1:T(8,128)(2,1)S(1)}, bf16[4,3,256,128]{3,2,0,1:T(8,128)(2,1)}, u32[]{:S(2)}) copy-start(bf16[4,3,256,128]{3,2,0,1:T(8,128)(2,1)} %get-tuple-element.557) | copy-start | bytes 2359300 | tf_op jit(solution)/shard_map/while
  266.2 4.0 copy-start.8
  270.2 12.6 %copy-start.6 = (bf16[4,3,256,128]{3,0,2,1:T(4,128)(2,1)S(1)}, bf16[4,3,256,128]{3,0,2,1:T(4,128)(2,1)}, u32[]{:S(2)}) copy-start(bf16[4,3,256,128]{3,0,2,1:T(4,128)(2,1)} %copy-done.5) | copy-start | bytes 2359300 | tf_op jit(solution)/shard_map/while
  282.8 20.9 %copy-start.10 = (bf16[4,3,256,128]{2,3,0,1:T(8,128)(2,1)S(1)}, bf16[4,3,256,128]{2,3,0,1:T(8,128)(2,1)}, u32[]{:S(2)}) copy-start(bf16[4,3,256,128]{2,3,0,1:T(8,128)(2,1)} %get-tuple-element.365) | copy-start | bytes 2359300
  282.8 22.1 %copy-start.9 = (bf16[4,3,256,128]{3,2,0,1:T(8,128)(2,1)S(1)}, bf16[4,3,256,128]{3,2,0,1:T(8,128)(2,1)}, u32[]{:S(2)}) copy-start(bf16[4,3,256,128]{3,2,0,1:T(8,128)(2,1)} %get-tuple-element.366) | copy-start | bytes 2359300
  290.0 72.7 %collective-permute-start.4 = (bf16[2,4,3,256,128]{4,3,2,1,0:T(8,128)(2,1)}, bf16[2,4,3,256,128]{4,3,2,1,0:T(8,128)(2,1)}, u32[]{:S(2)}, u32[]{:S(2)}) collective-permute-start(bf16[2,4,3,256,128]{4,3,2,1,0:T(8,128)(2,1)} %get-tuple-element.453), channel_id=1, source_target_pairs={{8,0},{12,4},{16,8},{20,12},{24,16},{28,20},{32,24},{36,28},{40,32... | collective-permute-start | bytes 4718600 | tf_op jit(solution)/shard_map/ppermute | solution.py:13
  294.3 68.5 %collective-permute-start.7 = (bf16[2,4,3,256,128]{4,3,2,1,0:T(8,128)(2,1)}, bf16[2,4,3,256,128]{4,3,2,1,0:T(8,128)(2,1)}, u32[]{:S(2)}, u32[]{:S(2)}) collective-permute-start(bf16[2,4,3,256,128]{4,3,2,1,0:T(8,128)(2,1)} %get-tuple-element.454), channel_id=1, source_target_pairs={{0,8},{4,12},{8,16},{12,20},{16,24},{20,28},{24,32},{28,36},{32,40... | collective-permute-start | bytes 4718600 | tf_op jit(solution)/shard_map/ppermute | solution.py:13
  296.3 103.5 %collective-permute-start.6 = (bf16[2,4,3,256,128]{4,3,2,1,0:T(8,128)(2,1)}, bf16[2,4,3,256,128]{4,3,2,1,0:T(8,128)(2,1)}, u32[]{:S(2)}, u32[]{:S(2)}) collective-permute-start(bf16[2,4,3,256,128]{4,3,2,1,0:T(8,128)(2,1)} %get-tuple-element.455), channel_id=1, source_target_pairs={{0,4},{4,8},{8,12},{12,16},{16,20},{20,24},{24,28},{28,32},{32,36}... | collective-permute-start | bytes 4718600 | tf_op jit(solution)/shard_map/ppermute | solution.py:13
  298.6 101.1 %collective-permute-start.5 = (bf16[2,4,3,256,128]{4,3,2,1,0:T(8,128)(2,1)S(1)}, bf16[2,4,3,256,128]{4,3,2,1,0:T(8,128)(2,1)}, u32[]{:S(2)}, u32[]{:S(2)}) collective-permute-start(bf16[2,4,3,256,128]{4,3,2,1,0:T(8,128)(2,1)S(1)} %get-tuple-element.456), channel_id=1, source_target_pairs={{4,0},{8,4},{12,8},{16,12},{20,16},{24,20},{28,24},{32,28},{36,32}... | collective-permute-start | bytes 4718600 | tf_op jit(solution)/shard_map/ppermute | solution.py:13
where the time goes:
time: 416 us; the launch traced here: 408 us
  waiting for transfers between devices  167 us (40%)
  local copies, waits for them, and re-layouts  90.4 us (22%)
  matrix products  57.5 us (14%)
  other arithmetic  50.1 us (12%)
  starting transfers between devices  34.9 us (8%)
  loops' own time  7.99 us (2%)
    ppermute x8, waiting for transfers between devices, from_behind(): lax.ppermute(value, axis, [(source, source + steps) for source in range(f...  138 us
    dynamic_update_slice x3, other arithmetic, visit(): lax.dynamic_update_slice(partial_value, lax.dynamic_slice(partial_value,...  37.7 us
    ppermute x8, starting transfers between devices, from_behind(): lax.ppermute(value, axis, [(source, source + steps) for source in range(f...  29.1 us
    all_to_all x1, waiting for transfers between devices, shards(): lax.all_to_all(grad_out, 'head', split_axis=3, concat_axis=2, tiled=True)  28.2 us
    while x36, local copies, waits for them, and re-layouts  22 us
    unnamed x25, local copies, waits for them, and re-layouts  19.5 us
    slice x3, local copies, waits for them, and re-layouts, visit(): block[0]  15.5 us
    dot_general x3, matrix products, key_terms(): jnp.einsum('hqk,hqd->hkd', weights, grad, preferred_element_type=jnp.floa...  13.9 us
  transfers between devices with their start and end apart: 9, of which 4 were waited for; matrix products, arithmetic and copies ran while one was open for 6% of the time, Pallas kernels for 0%

commit v1 on v0

v1 whole, which is shorter than its diff:
```python
import functools

import jax
import jax.numpy as jnp
from jax import lax
from jax.experimental import pallas as pl
from jax.experimental.pallas import tpu as pltpu
from jax.sharding import PartitionSpec as P

DH = 128
WIN = 3
SLOTS = 2 * WIN - 1
OWN = WIN - 1
SCALE = DH ** (-0.5)
LOG2E = 1.4426950408889634
MESH = pl.DeviceIdType.MESH
F32 = jnp.float32
BF16 = jnp.bfloat16

NT = (((1,), (1,)), ((), ()))


def dot_nt(a, b):
    return lax.dot_general(a, b, NT, preferred_element_type=F32)


def dot_nn(a, b):
    return jnp.dot(a, b, preferred_element_type=F32)


def fold(block, op):
    rows, lanes = block.shape
    return op(block.reshape(rows // 8, 8, lanes), axis=0)


def kernel(
    heads,
    times,
    tile,
    groups,
    start_ref,
    count_ref,
    q_hbm,
    k_hbm,
    v_hbm,
    g_hbm,
    att_hbm,
    dq_hbm,
    dk_hbm,
    dv_hbm,
    kv,
    far_out,
    far_in,
    near_out,
    near_in,
    near_sum,
    own_sum,
    q_buf,
    g_buf,
    att_buf,
    dq_buf,
    dk_buf,
    dv_buf,
    k_cur,
    v_cur,
    kt_cur,
    vt_cur,
    s_buf,
    dp_buf,
    w_buf,
    ds_buf,
    load_sem,
    g_here,
    g_send,
    g_recv,
    own_send,
    own_recv,
    relay_send,
    relay_recv,
    far_send,
    far_recv,
    near_send,
    near_recv,
    out_sem,
):
    count = lax.axis_size("ctx")
    here = lax.axis_index("ctx")
    group = lax.axis_index("head")
    left = lax.rem(here + count - 1, count)
    right = lax.rem(here + 1, count)
    toward = (left, right)
    part = tile // groups
    chunks = WIN * times

    def lanes(head):
        return pl.ds(pl.multiple_of(head * DH, DH), DH)

    def load(which, head):
        source, target = (
            (k_hbm, kv.at[head, OWN, 0]),
            (v_hbm, kv.at[head, OWN, 1]),
            (q_hbm, q_buf.at[head]),
        )[which]
        return pltpu.make_async_copy(
            source.at[:, :, lanes(head)], target, load_sem.at[head, which]
        )

    def remote(source, target, sends, recvs, head, side):
        return pltpu.make_async_remote_copy(
            src_ref=source,
            dst_ref=target,
            send_sem=sends.at[head, side],
            recv_sem=recvs.at[head, side],
            device_id=(toward[side], group),
            device_id_type=MESH,
        )

    def own_copy(head, side):
        slot = OWN + 1 if side == 0 else OWN - 1
        return remote(kv.at[head, OWN], kv.at[head, slot], own_send, own_recv, head, side)

    def relay_copy(head, side):
        slot = OWN + 1 if side == 0 else OWN - 1
        target = OWN + 2 if side == 0 else OWN - 2
        return remote(kv.at[head, slot], kv.at[head, target], relay_send, relay_recv, head, side)

    def far_copy(head, side):
        return remote(
            far_out.at[head, side], far_in.at[head, side], far_send, far_recv, head, side
        )

    def near_copy(head, side):
        return remote(
            near_out.at[head, side], near_in.at[head, side], near_send, near_recv, head, side
        )

    def grad_copy(step, head):
        peer = lax.rem(group + step, groups)
        return pltpu.make_async_remote_copy(
            src_ref=g_hbm.at[:, :, lanes(peer * heads + head)],
            dst_ref=g_buf.at[head, :, pl.ds(pl.multiple_of(group * part, part), part), :],
            send_sem=g_send.at[step, head],
            recv_sem=g_recv.at[step, head],
            device_id=(here, peer),
            device_id_type=MESH,
        )

    def grad_here(head):
        return pltpu.make_async_copy(
            g_hbm.at[:, :, lanes(group * heads + head)],
            g_buf.at[head, :, pl.ds(pl.multiple_of(group * part, part), part), :],
            g_here.at[head],
        )

    def out_copy(which, head):
        source, target = (
            (att_buf, att_hbm),
            (dq_buf, dq_hbm),
            (dk_buf, dk_hbm),
            (dv_buf, dv_hbm),
        )[which]
        return pltpu.make_async_copy(
            source.at[head], target.at[:, :, lanes(head)], out_sem.at[which, head]
        )

    for head in range(heads):
        for which in range(3):
            load(which, head).start()
    for head in range(heads):
        grad_here(head).start()

    barrier = pltpu.get_barrier_semaphore()
    for neighbour in toward:
        pl.semaphore_signal(barrier, inc=1, device_id=(neighbour, group), device_id_type=MESH)
    for step in range(1, groups):
        pl.semaphore_signal(
            barrier,
            inc=1,
            device_id=(here, lax.rem(group + step, groups)),
            device_id_type=MESH,
        )
    pl.semaphore_wait(barrier, 2 + groups - 1)

    def send_own(head):
        load(0, head).wait()
        load(1, head).wait()
        for side in range(2):
            own_copy(head, side).start()

    def send_relay(head):
        for side in (1, 0):
            own_copy(head, side).wait_recv()
            relay_copy(head, side).start()

    send_own(0)
    for step in range(1, groups):
        grad_copy(step, 0).start()
    send_own(1)
    for head in range(1, heads):
        for step in range(1, groups):
            grad_copy(step, head).start()

    zero_tile = jnp.zeros((tile, tile), BF16)
    for t in range(times):
        for j in range(times):
            w_buf[t, WIN, j] = zero_tile
            ds_buf[t, WIN, j] = zero_tile
    row = lax.broadcasted_iota(jnp.int32, (tile, tile), 0)

    send_relay(0)
    if heads > 2:
        send_own(2)
    send_relay(1)
    for head in range(3, heads):
        send_own(head)

    def tile_step(head, t):
        start = jnp.clip(start_ref[here, t], 0, count - WIN)
        rel = jnp.clip(start - here + OWN, 0, OWN)
        q = q_buf[head, t]
        g = g_buf[head, t]

        def place(i):
            return i // times, i % times

        def scores(i, top):
            s, j = place(i)
            block = dot_nt(k_cur[rel + s, j], q) * (SCALE * LOG2E)
            block = jnp.where(row < count_ref[start + s, j], block, -jnp.inf)
            s_buf[i] = block
            return jnp.maximum(top, fold(block, jnp.max))

        top = lax.fori_loop(0, chunks, scores, jnp.full((8, tile), -jnp.inf, F32))
        top = jnp.max(top, axis=0, keepdims=True)

        def exps(i, total):
            s, j = place(i)
            block = jnp.exp2(s_buf[i] - top)
            s_buf[i] = block
            dp_buf[i] = dot_nt(v_cur[rel + s, j], g)
            return total + fold(block, jnp.sum)

        total = lax.fori_loop(0, chunks, exps, jnp.zeros((8, tile), F32))
        inverse = 1.0 / jnp.sum(total, axis=0, keepdims=True)

        def attend(i, att):
            s, j = place(i)
            probs = s_buf[i] * inverse
            s_buf[i] = probs
            weights = probs.astype(BF16)
            w_buf[t, s, j] = weights
            return att + dot_nn(vt_cur[rel + s, j], weights)

        att = lax.fori_loop(0, chunks, attend, jnp.zeros((DH, tile), F32))
        rounded = att.astype(BF16).astype(F32)
        att_buf[head, t] = rounded.T.astype(BF16)
        delta = jnp.sum(g.astype(F32).T * rounded, axis=0, keepdims=True)

        def back(i, dq):
            s, j = place(i)
            dscores = (s_buf[i] * (dp_buf[i] - delta)).astype(BF16)
            ds_buf[t, s, j] = dscores
            return dq + dot_nn(kt_cur[rel + s, j], dscores)

        dq = lax.fori_loop(0, chunks, back, jnp.zeros((DH, tile), F32))
        dq_buf[head, t] = (dq * SCALE).T.astype(BF16)

    def key_side(head):
        rels = [jnp.clip(start_ref[here, t] - here + OWN, 0, OWN) for t in range(times)]

        def parts(slot, j):
            dk = jnp.zeros((tile, DH), F32)
            dv = jnp.zeros((tile, DH), F32)
            for t in range(times):
                s = slot - rels[t]
                s = jnp.where((s >= 0) & (s < WIN), s, WIN)
                dk = dk + dot_nn(ds_buf[t, s, j], q_buf[head, t])
                dv = dv + dot_nn(w_buf[t, s, j], g_buf[head, t])
            return dk * SCALE, dv

        for slot in (0, SLOTS - 1, 1, SLOTS - 2, OWN):

            def one(j, carry, slot=slot):
                pair = parts(slot, j)
                for which in range(2):
                    if slot == 0:
                        far_out[head, 0, which, j] = pair[which].astype(BF16)
                    elif slot == SLOTS - 1:
                        far_out[head, 1, which, j] = pair[which].astype(BF16)
                    elif slot == OWN:
                        own_sum[head, which, j] = pair[which]
                    else:
                        near_sum[head, 0 if slot < OWN else 1, which, j] = pair[which]
                return carry

            lax.fori_loop(0, times, one, 0)
            if slot in (0, SLOTS - 1):
                side = 0 if slot == 0 else 1

                @pl.when(head > 0)
                def _():
                    far_copy(head, side).start()

    def send_near(head):
        for side in range(2):
            far_copy(head, side).wait_recv()
            for which in range(2):

                def one(j, carry, which=which, side=side):
                    near_out[head, side, which, j] = (
                        near_sum[head, side, which, j]
                        + far_in[head, side, which, j].astype(F32)
                    ).astype(BF16)
                    return carry

                lax.fori_loop(0, times, one, 0)
            near_copy(head, side).start()

    def finish(head):
        for side in range(2):
            near_copy(head, side).wait_recv()

        def one(j, carry):
            for which, out in enumerate((dk_buf, dv_buf)):
                out[head, j] = (
                    own_sum[head, which, j]
                    + near_in[head, 0, which, j].astype(F32)
                    + near_in[head, 1, which, j].astype(F32)
                ).astype(BF16)
            return carry

        lax.fori_loop(0, times, one, 0)
        out_copy(2, head).start()
        out_copy(3, head).start()

    def head_step(head, carry):
        load(2, head).wait()
        grad_here(head).wait()
        for step in range(1, groups):
            grad_copy(step, head).wait_recv()
        for side in range(2):
            relay_copy(head, side).wait_recv()

        def stage(i, inner):
            slot, j = i // times, i % times
            keys = kv[head, slot, 0, j]
            values = kv[head, slot, 1, j]
            k_cur[slot, j] = keys
            v_cur[slot, j] = values
            kt_cur[slot, j] = keys.T
            vt_cur[slot, j] = values.T
            return inner

        lax.fori_loop(0, SLOTS * times, stage, 0)

        def visit(t, inner):
            tile_step(head, t)
            return inner

        lax.fori_loop(0, times, visit, 0)
        out_copy(0, head).start()
        out_copy(1, head).start()
        key_side(head)

        @pl.when(head == 0)
        def _():
            for later in range(2, heads):
                send_relay(later)
            for side in range(2):
                far_copy(head, side).start()

        @pl.when(head > 0)
        def _():
            send_near(head - 1)

        @pl.when(head > 1)
        def _():
            finish(head - 2)

        return carry

    lax.fori_loop(0, heads, head_step, 0)
    send_near(heads - 1)
    finish(heads - 2)
    finish(heads - 1)

    def drain(head, carry):
        for side in range(2):
            own_copy(head, side).wait_send()
            relay_copy(head, side).wait_send()
            far_copy(head, side).wait_send()
            near_copy(head, side).wait_send()
        for step in range(1, groups):
            grad_copy(step, head).wait_send()
        for which in range(4):
            out_copy(which, head).wait()
        return carry

    lax.fori_loop(0, heads, drain, 0)


def shards(queries, keys, values, grad_out, window_start, key_counts):
    _, times, tile, width = queries.shape
    heads = width // DH
    groups = tile // grad_out.shape[2]
    block = (times, tile, DH)
    dma = pltpu.SemaphoreType.DMA
    any_spec = pl.BlockSpec(memory_space=pl.ANY)
    smem_spec = pl.BlockSpec(memory_space=pltpu.SMEM)
    out = jax.ShapeDtypeStruct((times, tile, width), BF16)
    pairs = times * heads * 6 * tile * WIN * times * tile * DH * 2
    results = pl.pallas_call(
        functools.partial(kernel, heads, times, tile, groups),
        out_shape=(out,) * 4,
        in_specs=[smem_spec, smem_spec] + [any_spec] * 4,
        out_specs=(any_spec,) * 4,
        scratch_shapes=[
            pltpu.VMEM((heads, SLOTS, 2) + block, BF16),
            pltpu.VMEM((heads, 2, 2) + block, BF16),
            pltpu.VMEM((heads, 2, 2) + block, BF16),
            pltpu.VMEM((heads, 2, 2) + block, BF16),
            pltpu.VMEM((heads, 2, 2) + block, BF16),
            pltpu.VMEM((heads, 2, 2) + block, F32),
            pltpu.VMEM((heads, 2) + block, F32),
            pltpu.VMEM((heads,) + block, BF16),
            pltpu.VMEM((heads,) + block, BF16),
            pltpu.VMEM((heads,) + block, BF16),
            pltpu.VMEM((heads,) + block, BF16),
            pltpu.VMEM((heads,) + block, BF16),
            pltpu.VMEM((heads,) + block, BF16),
            pltpu.VMEM((SLOTS, times, tile, DH), BF16),
            pltpu.VMEM((SLOTS, times, tile, DH), BF16),
            pltpu.VMEM((SLOTS, times, DH, tile), BF16),
            pltpu.VMEM((SLOTS, times, DH, tile), BF16),
            pltpu.VMEM((WIN * times, tile, tile), F32),
            pltpu.VMEM((WIN * times, tile, tile), F32),
            pltpu.VMEM((times, WIN + 1, times, tile, tile), BF16),
            pltpu.VMEM((times, WIN + 1, times, tile, tile), BF16),
            dma((heads, 3)),
            dma((heads,)),
            dma((groups, heads)),
            dma((groups, heads)),
            dma((heads, 2)),
            dma((heads, 2)),
            dma((heads, 2)),
            dma((heads, 2)),
            dma((heads, 2)),
            dma((heads, 2)),
            dma((heads, 2)),
            dma((heads, 2)),
            dma((4, heads)),
        ],
        compiler_params=pltpu.CompilerParams(
            collective_id=0, has_side_effects=True, vmem_limit_bytes=60 * 1024 * 1024
        ),
        cost_estimate=pl.CostEstimate(
            flops=pairs, bytes_accessed=8 * times * tile * width * 2, transcendentals=0
        ),
        name="band_attention",
    )(window_start, key_counts, queries[0], keys[0], values[0], grad_out[0])
    return tuple(result[None] for result in results)


def solution(mesh):
    placed = (
        P("ctx", None, None, "head"),
        P("ctx", None, None, "head"),
        P("ctx", None, None, "head"),
        P("ctx", None, "head", None),
        P(),
        P(),
    )
    return jax.shard_map(
        shards,
        mesh=mesh,
        in_specs=placed,
        out_specs=(P("ctx", None, None, "head"),) * 4,
        check_vma=False,
    )
```

time: 416 us -> 213 us (0.51); the launches traced: 408 us -> 212 us
  Pallas kernels: 0 us -> 204 us
  waiting for transfers between devices: 167 us -> 0 us
  local copies, waits for them, and re-layouts: 90.4 us -> 7.95 us
  matrix products: 57.5 us -> 0 us
  other arithmetic: 50.1 us -> 0 us
  starting transfers between devices: 34.9 us -> 0 us
  loops' own time: 7.99 us -> 0 us
    pallas_call x0 -> x1, Pallas kernels: none -> 204 us  [shards(): pl.pallas_call(functools.partial(kernel, heads, times, tile, groups), out...]
    ppermute x8 -> x0, waiting for transfers between devices: 138 us -> none  [from_behind(): lax.ppermute(value, axis, [(source, source + steps) for source in range(f...]
    dot_general x18 -> x0, matrix products: 57.5 us -> none  [the longest x3 13.9 us: key_terms(): jnp.einsum('hqk,hqd->hkd', weights, grad, preferred_element_type=jnp.floa...]
    dynamic_update_slice x3 -> x0, other arithmetic: 37.7 us -> none  [visit(): lax.dynamic_update_slice(partial_value, lax.dynamic_slice(partial_value,...]
    ppermute x8 -> x0, starting transfers between devices: 29.1 us -> none  [from_behind(): lax.ppermute(value, axis, [(source, source + steps) for source in range(f...]
    all_to_all x1 -> x0, waiting for transfers between devices: 28.2 us -> none  [shards(): lax.all_to_all(grad_out, 'head', split_axis=3, concat_axis=2, tiled=True)]
    while x36 -> x0, local copies, waits for them, and re-layouts: 22 us -> none
    slice x3 -> x0, local copies, waits for them, and re-layouts: 15.5 us -> none  [visit(): block[0]]
  transfers between devices with their start and end apart: 9 -> 0, of which waited for: 4 -> 0; matrix products, arithmetic and copies ran while one was open for 6% -> 0% of each run, Pallas kernels for 0% -> 0%
where the time goes in v1:
time: 213 us; the launch traced here: 212 us
  Pallas kernels  204 us (96%)
  local copies, waits for them, and re-layouts  7.95 us (4%)
    pallas_call x1, Pallas kernels, shards(): pl.pallas_call(functools.partial(kernel, heads, times, tile, groups), out...  204 us
    unnamed x16, local copies, waits for them, and re-layouts  7.95 us

profile of v1, /device:TPU:25, one launch (start us, length us, event | category | flops | bytes accessed | tf_op | source)
XLA Modules:
  0.0 212.3 jit_solution(4972503419669274696)
XLA Ops:
  0.6 0.0 copy-start.3
  0.6 0.7 copy-done.3
  1.3 0.0 copy-start.4
  1.3 0.7 copy.10.start_ref
  2.0 0.0 copy-done.4
  2.0 0.7 copy.11.count_ref
  2.7 203.7 %band_attention.1 = (bf16[3,256,512]{2,1,0:T(8,128)(2,1)}, bf16[3,256,512]{2,1,0:T(8,128)(2,1)}, bf16[3,256,512]{2,1,0:T(8,128)(2,1)}, bf16[3,256,512]{2,1,0:T(8,128)(2,1)}) custom-call(s32[64,3]{1,0:T(8,128)} %copy.10.start_ref, s32[64,3]{1,0:T(8,128)} %copy.11.count_ref, bf16[3,256,512]{2,1,0:T(8,128)(2,1)} %bitcast.12, bf16[3,256,512]{2,1,0:T(8,128)(2,1)} %bitcast.13, ...), custom_call_target="tpu_custom_call" | custom-call | flops 10871635968 | bytes 6291456 | tf_op jit(solution)/shard_map/band_attention/pallas_call | solution.py:412
  206.5 0.0 copy-start.2
  206.5 2.1 %copy.16 = bf16[1,3,256,512]{3,2,1,0:T(8,128)(2,1)} copy(bf16[1,3,256,512]{3,2,1,0:T(8,128)(2,1)} %bitcast.11) | data formatting | bytes 1572864
  208.6 0.0 copy-done.2
  208.6 0.0 copy-start.1
  208.6 0.9 copy.17
  209.5 0.5 copy-done.1
  210.0 0.0 copy-start
  210.0 0.9 copy.18
  210.9 0.5 copy-done
  211.4 0.9 copy.19
Async XLA Ops:
  0.6 0.7 copy-start.3
  1.3 0.7 copy-start.4
  206.5 2.1 %copy-start.2 = (bf16[3,256,512]{2,1,0:T(8,128)(2,1)S(1)}, bf16[3,256,512]{2,1,0:T(8,128)(2,1)}, u32[]{:S(2)}) copy-start(bf16[3,256,512]{2,1,0:T(8,128)(2,1)} %get-tuple-element.9) | copy-start | bytes 2359300
  208.6 1.4 copy-start.1
  210.0 1.4 copy-start

commit v2 on v1

--- a/solution.py
+++ b/solution.py
@@ -26,6 +26,10 @@
 
 def dot_nn(a, b):
     return jnp.dot(a, b, preferred_element_type=F32)
+
+
+def looped(unroll, count, body, carry):
+    return lax.fori_loop(0, count, body, carry, unroll=unroll)
 
 
 def fold(block, op):
@@ -91,6 +95,7 @@
     toward = (left, right)
     part = tile // groups
     chunks = WIN * times
+    width = heads * DH
 
     def lanes(head):
         return pl.ds(pl.multiple_of(head * DH, DH), DH)
@@ -134,23 +139,25 @@
             near_out.at[head, side], near_in.at[head, side], near_send, near_recv, head, side
         )
 
-    def grad_copy(step, head):
+    def grad_rows():
+        return g_buf.at[:, pl.ds(pl.multiple_of(group * part, part), part), :]
+
+    def grad_lanes(owner):
+        return g_hbm.at[:, :, pl.ds(pl.multiple_of(owner * width, width), width)]
+
+    def grad_copy(step):
         peer = lax.rem(group + step, groups)
         return pltpu.make_async_remote_copy(
-            src_ref=g_hbm.at[:, :, lanes(peer * heads + head)],
-            dst_ref=g_buf.at[head, :, pl.ds(pl.multiple_of(group * part, part), part), :],
-            send_sem=g_send.at[step, head],
-            recv_sem=g_recv.at[step, head],
+            src_ref=grad_lanes(peer),
+            dst_ref=grad_rows(),
+            send_sem=g_send.at[step],
+            recv_sem=g_recv.at[step],
             device_id=(here, peer),
             device_id_type=MESH,
         )
 
-    def grad_here(head):
-        return pltpu.make_async_copy(
-            g_hbm.at[:, :, lanes(group * heads + head)],
-            g_buf.at[head, :, pl.ds(pl.multiple_of(group * part, part), part), :],
-            g_here.at[head],
-        )
+    def grad_here():
+        return pltpu.make_async_copy(grad_lanes(group), grad_rows(), g_here)
 
     def out_copy(which, head):
         source, target = (
@@ -166,8 +173,7 @@
     for head in range(heads):
         for which in range(3):
             load(which, head).start()
-    for head in range(heads):
-        grad_here(head).start()
+    grad_here().start()
 
     barrier = pltpu.get_barrier_semaphore()
     for neighbour in toward:
@@ -192,13 +198,13 @@
             own_copy(head, side).wait_recv()
             relay_copy(head, side).start()
 
+    for step in range(1, groups):
+        grad_copy(step).start()
+    grad_here().wait()
+    for step in range(1, groups):
+        grad_copy(step).wait_recv()
     send_own(0)
-    for step in range(1, groups):
-        grad_copy(step, 0).start()
     send_own(1)
-    for head in range(1, heads):
-        for step in range(1, groups):
-            grad_copy(step, head).start()
 
     zero_tile = jnp.zeros((tile, tile), BF16)
     for t in range(times):
@@ -218,7 +224,7 @@
         start = jnp.clip(start_ref[here, t], 0, count - WIN)
         rel = jnp.clip(start - here + OWN, 0, OWN)
         q = q_buf[head, t]
-        g = g_buf[head, t]
+        g = g_buf[t, :, lanes(head)]
 
         def place(i):
             return i // times, i % times
@@ -230,7 +236,7 @@
             s_buf[i] = block
             return jnp.maximum(top, fold(block, jnp.max))
 
-        top = lax.fori_loop(0, chunks, scores, jnp.full((8, tile), -jnp.inf, F32))
+        top = looped(9, chunks, scores, jnp.full((8, tile), -jnp.inf, F32))
         top = jnp.max(top, axis=0, keepdims=True)
 
         def exps(i, total):
@@ -240,7 +246,7 @@
             dp_buf[i] = dot_nt(v_cur[rel + s, j], g)
             return total + fold(block, jnp.sum)
 
-        total = lax.fori_loop(0, chunks, exps, jnp.zeros((8, tile), F32))
+        total = looped(9, chunks, exps, jnp.zeros((8, tile), F32))
         inverse = 1.0 / jnp.sum(total, axis=0, keepdims=True)
 
         def attend(i, att):
@@ -251,7 +257,7 @@
             w_buf[t, s, j] = weights
             return att + dot_nn(vt_cur[rel + s, j], weights)
 
-        att = lax.fori_loop(0, chunks, attend, jnp.zeros((DH, tile), F32))
+        att = looped(9, chunks, attend, jnp.zeros((DH, tile), F32))
         rounded = att.astype(BF16).astype(F32)
         att_buf[head, t] = rounded.T.astype(BF16)
         delta = jnp.sum(g.astype(F32).T * rounded, axis=0, keepdims=True)
@@ -262,7 +268,7 @@
             ds_buf[t, s, j] = dscores
             return dq + dot_nn(kt_cur[rel + s, j], dscores)
 
-        dq = lax.fori_loop(0, chunks, back, jnp.zeros((DH, tile), F32))
+        dq = looped(9, chunks, back, jnp.zeros((DH, tile), F32))
         dq_buf[head, t] = (dq * SCALE).T.astype(BF16)
 
     def key_side(head):
@@ -275,7 +281,7 @@
                 s = slot - rels[t]
                 s = jnp.where((s >= 0) & (s < WIN), s, WIN)
                 dk = dk + dot_nn(ds_buf[t, s, j], q_buf[head, t])
-                dv = dv + dot_nn(w_buf[t, s, j], g_buf[head, t])
+                dv = dv + dot_nn(w_buf[t, s, j], g_buf[t, :, lanes(head)])
             return dk * SCALE, dv
 
         for slot in (0, SLOTS - 1, 1, SLOTS - 2, OWN):
@@ -293,7 +299,7 @@
                         near_sum[head, 0 if slot < OWN else 1, which, j] = pair[which]
                 return carry
 
-            lax.fori_loop(0, times, one, 0)
+            lax.fori_loop(0, times, one, 0, unroll=True)
             if slot in (0, SLOTS - 1):
                 side = 0 if slot == 0 else 1
 
@@ -335,9 +341,7 @@
 
     def head_step(head, carry):
         load(2, head).wait()
-        grad_here(head).wait()
-        for step in range(1, groups):
-            grad_copy(step, head).wait_recv()
+
         for side in range(2):
             relay_copy(head, side).wait_recv()
 
@@ -390,13 +394,13 @@
             relay_copy(head, side).wait_send()
             far_copy(head, side).wait_send()
             near_copy(head, side).wait_send()
-        for step in range(1, groups):
-            grad_copy(step, head).wait_send()
         for which in range(4):
             out_copy(which, head).wait()
         return carry
 
     lax.fori_loop(0, heads, drain, 0)
+    for step in range(1, groups):
+        grad_copy(step).wait_send()
 
 
 def shards(queries, keys, values, grad_out, window_start, key_counts):
@@ -423,7 +427,7 @@
             pltpu.VMEM((heads, 2, 2) + block, F32),
             pltpu.VMEM((heads, 2) + block, F32),
             pltpu.VMEM((heads,) + block, BF16),
-            pltpu.VMEM((heads,) + block, BF16),
+            pltpu.VMEM((times, tile, width), BF16),
             pltpu.VMEM((heads,) + block, BF16),
             pltpu.VMEM((heads,) + block, BF16),
             pltpu.VMEM((heads,) + block, BF16),
@@ -437,9 +441,9 @@
             pltpu.VMEM((times, WIN + 1, times, tile, tile), BF16),
             pltpu.VMEM((times, WIN + 1, times, tile, tile), BF16),
             dma((heads, 3)),
-            dma((heads,)),
-            dma((groups, heads)),
-            dma((groups, heads)),
+            dma,
+            dma((groups,)),
+            dma((groups,)),
             dma((heads, 2)),
             dma((heads, 2)),
             dma((heads, 2)),

time: 213 us -> 169 us (0.79)
  the two profiles are of different devices: /device:TPU:25 before, /device:TPU:1 now
where the time goes in v2:
time: 169 us; the launch traced here: 168 us
  Pallas kernels  159 us (94%)
  local copies, waits for them, and re-layouts  7.95 us (5%)
    pallas_call x1, Pallas kernels, shards(): pl.pallas_call(functools.partial(kernel, heads, times, tile, groups), out...  159 us
    unnamed x16, local copies, waits for them, and re-layouts  7.95 us

profile of v2, /device:TPU:1, one launch (start us, length us, event | category | flops | bytes accessed | tf_op | source)
XLA Modules:
  0.0 168.1 jit_solution(4303678209985855138)
XLA Ops:
  0.6 0.0 copy-start.3
  0.6 0.7 copy-done.3
  1.3 0.0 copy-start.4
  1.3 0.7 copy.10.start_ref
  2.0 0.0 copy-done.4
  2.0 0.7 copy.11.count_ref
  2.7 159.5 %band_attention.1 = (bf16[3,256,512]{2,1,0:T(8,128)(2,1)}, bf16[3,256,512]{2,1,0:T(8,128)(2,1)}, bf16[3,256,512]{2,1,0:T(8,128)(2,1)}, bf16[3,256,512]{2,1,0:T(8,128)(2,1)}) custom-call(s32[64,3]{1,0:T(8,128)} %copy.10.start_ref, s32[64,3]{1,0:T(8,128)} %copy.11.count_ref, bf16[3,256,512]{2,1,0:T(8,128)(2,1)} %bitcast.12, bf16[3,256,512]{2,1,0:T(8,128)(2,1)} %bitcast.13, ...), custom_call_target="tpu_custom_call" | custom-call | flops 10871635968 | bytes 6291456 | tf_op jit(solution)/shard_map/band_attention/pallas_call | solution.py:416
  162.2 0.0 copy-start.2
  162.2 2.1 %copy.16 = bf16[1,3,256,512]{3,2,1,0:T(8,128)(2,1)} copy(bf16[1,3,256,512]{3,2,1,0:T(8,128)(2,1)} %bitcast.11) | data formatting | bytes 1572864
  164.4 0.0 copy-done.2
  164.4 0.0 copy-start.1
  164.4 0.9 copy.17
  165.3 0.5 copy-done.1
  165.8 0.0 copy-start
  165.8 0.9 copy.18
  166.7 0.5 copy-done
  167.2 0.9 copy.19
Async XLA Ops:
  0.6 0.7 copy-start.3
  1.3 0.7 copy-start.4
  162.2 2.1 %copy-start.2 = (bf16[3,256,512]{2,1,0:T(8,128)(2,1)S(1)}, bf16[3,256,512]{2,1,0:T(8,128)(2,1)}, u32[]{:S(2)}) copy-start(bf16[3,256,512]{2,1,0:T(8,128)(2,1)} %get-tuple-element.9) | copy-start | bytes 2359300
  164.4 1.4 copy-start.1
  165.8 1.4 copy-start

commit v3 on v2

--- a/solution.py
+++ b/solution.py
@@ -221,7 +221,7 @@
         send_own(head)
 
     def tile_step(head, t):
-        start = jnp.clip(start_ref[here, t], 0, count - WIN)
+        start = jnp.clip(start_ref[t, here], 0, count - WIN)
         rel = jnp.clip(start - here + OWN, 0, OWN)
         q = q_buf[head, t]
         g = g_buf[t, :, lanes(head)]
@@ -232,7 +232,7 @@
         def scores(i, top):
             s, j = place(i)
             block = dot_nt(k_cur[rel + s, j], q) * (SCALE * LOG2E)
-            block = jnp.where(row < count_ref[start + s, j], block, -jnp.inf)
+            block = jnp.where(row < count_ref[j, start + s], block, -jnp.inf)
             s_buf[i] = block
             return jnp.maximum(top, fold(block, jnp.max))
 
@@ -272,7 +272,7 @@
         dq_buf[head, t] = (dq * SCALE).T.astype(BF16)
 
     def key_side(head):
-        rels = [jnp.clip(start_ref[here, t] - here + OWN, 0, OWN) for t in range(times)]
+        rels = [jnp.clip(start_ref[t, here] - here + OWN, 0, OWN) for t in range(times)]
 
         def parts(slot, j):
             dk = jnp.zeros((tile, DH), F32)
@@ -401,6 +401,25 @@
     lax.fori_loop(0, heads, drain, 0)
     for step in range(1, groups):
         grad_copy(step).wait_send()
+
+
+def forward(times, *refs):
+    sources, targets = refs[:4], refs[4:8]
+    held, in_sem, out_sem = refs[8:]
+    pieces = [(i, t) for t in range(times) for i in range(4)]
+    inward = [
+        pltpu.make_async_copy(sources[i].at[t], held.at[i, t], in_sem.at[i, t]) for i, t in pieces
+    ]
+    outward = [
+        pltpu.make_async_copy(held.at[i, t], targets[i].at[t], out_sem.at[i, t]) for i, t in pieces
+    ]
+    for copy in inward:
+        copy.start()
+    for first, second in zip(inward, outward):
+        first.wait()
+        second.start()
+    for copy in outward:
+        copy.wait()
 
 
 def shards(queries, keys, values, grad_out, window_start, key_counts):
@@ -461,7 +480,19 @@
             flops=pairs, bytes_accessed=8 * times * tile * width * 2, transcendentals=0
         ),
         name="band_attention",
-    )(window_start, key_counts, queries[0], keys[0], values[0], grad_out[0])
+    )(window_start.T, key_counts.T, queries[0], keys[0], values[0], grad_out[0])
+    results = pl.pallas_call(
+        functools.partial(forward, times),
+        out_shape=(out,) * 4,
+        in_specs=[any_spec] * 4,
+        out_specs=(any_spec,) * 4,
+        scratch_shapes=[
+            pltpu.VMEM((4, times, tile, width), BF16),
+            dma((4, times)),
+            dma((4, times)),
+        ],
+        name="place_results",
+    )(*results)
     return tuple(result[None] for result in results)
 
 

time: 169 us -> 162 us (0.959)
  local copies, waits for them, and re-layouts: 7.95 us -> 0 us
  Pallas kernels: 159 us -> 161 us
    unnamed x16 -> x0, local copies, waits for them, and re-layouts: 7.95 us -> none
    pallas_call x0 -> x1, Pallas kernels: none -> 2.81 us  [shards(): pl.pallas_call(functools.partial(forward, times), out_shape=(out,) * 4, i...]
where the time goes in v3:
time: 162 us
  Pallas kernels  161 us (99%)
    pallas_call x1, Pallas kernels, shards(): pl.pallas_call(functools.partial(kernel, heads, times, tile, groups), out...  159 us

profile of v3, /device:TPU:1, one launch (start us, length us, event | category | flops | bytes accessed | tf_op | source)
XLA Modules:
  0.0 162.1 jit_solution(5386418523532156681)
XLA Ops:
  0.6 158.6 %band_attention.1 = (bf16[3,256,512]{2,1,0:T(8,128)(2,1)}, bf16[3,256,512]{2,1,0:T(8,128)(2,1)}, bf16[3,256,512]{2,1,0:T(8,128)(2,1)}, bf16[3,256,512]{2,1,0:T(8,128)(2,1)}) custom-call(s32[3,64]{1,0:T(4,128)} %bitcast.18, s32[3,64]{1,0:T(4,128)} %bitcast.19, bf16[3,256,512]{2,1,0:T(8,128)(2,1)} %bitcast.10, bf16[3,256,512]{2,1,0:T(8,128)(2,1)} %bitcast.11, ...), custom_call_target="tpu_custom_call" | custom-call | flops 10871635968 | bytes 6291456 | tf_op jit(solution)/shard_map/band_attention/pallas_call | solution.py:435
  159.2 2.8 %place_results.1 = (bf16[3,256,512]{2,1,0:T(8,128)(2,1)}, bf16[3,256,512]{2,1,0:T(8,128)(2,1)}, bf16[3,256,512]{2,1,0:T(8,128)(2,1)}, bf16[3,256,512]{2,1,0:T(8,128)(2,1)}) custom-call(bf16[3,256,512]{2,1,0:T(8,128)(2,1)} %get-tuple-element.12.refs_0_, bf16[3,256,512]{2,1,0:T(8,128)(2,1)} %get-tuple-element.13.refs_1_, ...), custom_call_target="tpu_custom_call" | custom-call | tf_op jit(solution)/shard_map/place_results/pallas_call | solution.py:484

commit v4 on v3

--- a/solution.py
+++ b/solution.py
@@ -11,6 +11,7 @@
 WIN = 3
 SLOTS = 2 * WIN - 1
 OWN = WIN - 1
+RUN = 8
 SCALE = DH ** (-0.5)
 LOG2E = 1.4426950408889634
 MESH = pl.DeviceIdType.MESH
@@ -35,6 +36,20 @@
 def fold(block, op):
     rows, lanes = block.shape
     return op(block.reshape(rows // 8, 8, lanes), axis=0)
+
+
+class Guarded:
+    def __init__(self, copy, sends, receives):
+        self.copy, self.sends, self.receives = copy, sends, receives
+
+    def start(self):
+        pl.when(self.sends)(lambda: self.copy.start())
+
+    def wait_send(self):
+        pl.when(self.sends)(lambda: self.copy.wait_send())
+
+    def wait_recv(self):
+        pl.when(self.receives)(lambda: self.copy.wait_recv())
 
 
 def kernel(
@@ -75,8 +90,13 @@
     ds_buf,
     load_sem,
     g_here,
-    g_send,
-    g_recv,
+    chip_send,
+    chip_recv,
+    cross_send,
+    cross_recv,
+    half_send,
+    half_recv,
+    g_mid,
     own_send,
     own_recv,
     relay_send,
@@ -95,6 +115,12 @@
     toward = (left, right)
     part = tile // groups
     chunks = WIN * times
+    pair, core = group // 2, group % 2
+    half = count // 2
+    partner = lax.rem(here + half, count)
+    flip = (here == half - RUN) | (here == half + RUN - 1)
+    special = flip | (here == RUN - 1) | (here == count - RUN)
+    next_pair = jnp.where(flip, 1 - pair, pair)
     width = heads * DH
 
     def lanes(head):
@@ -111,7 +137,7 @@
         )
 
     def remote(source, target, sends, recvs, head, side):
-        return pltpu.make_async_remote_copy(
+        copy = pltpu.make_async_remote_copy(
             src_ref=source,
             dst_ref=target,
             send_sem=sends.at[head, side],
@@ -119,6 +145,8 @@
             device_id=(toward[side], group),
             device_id_type=MESH,
         )
+        ends = (here > 0, here < count - 1)
+        return Guarded(copy, ends[side], ends[1 - side])
 
     def own_copy(head, side):
         slot = OWN + 1 if side == 0 else OWN - 1
@@ -139,25 +167,66 @@
             near_out.at[head, side], near_in.at[head, side], near_send, near_recv, head, side
         )
 
-    def grad_rows():
-        return g_buf.at[:, pl.ds(pl.multiple_of(group * part, part), part), :]
+    def grad_rows(owner):
+        return g_buf.at[:, pl.ds(pl.multiple_of(owner * part, part), part), :]
 
     def grad_lanes(owner):
         return g_hbm.at[:, :, pl.ds(pl.multiple_of(owner * width, width), width)]
 
-    def grad_copy(step):
-        peer = lax.rem(group + step, groups)
+    def grad_chip():
+        peer = pair * 2 + 1 - core
         return pltpu.make_async_remote_copy(
             src_ref=grad_lanes(peer),
-            dst_ref=grad_rows(),
-            send_sem=g_send.at[step],
-            recv_sem=g_recv.at[step],
+            dst_ref=grad_rows(group),
+            send_sem=chip_send,
+            recv_sem=chip_recv,
             device_id=(here, peer),
             device_id_type=MESH,
         )
 
+    def grad_cross(other):
+        peer = (1 - pair) * 2 + other
+        return pltpu.make_async_remote_copy(
+            src_ref=grad_lanes(peer),
+            dst_ref=grad_rows(group),
+            send_sem=cross_send.at[other],
+            recv_sem=cross_recv.at[core],
+            device_id=(here, peer),
+            device_id_type=MESH,
+        )
+
+    def grad_half(other):
+        return pltpu.make_async_remote_copy(
+            src_ref=grad_lanes((1 - pair) * 2 + other),
+            dst_ref=g_mid.at[other],
+            send_sem=half_send.at[other],
+            recv_sem=half_recv.at[other],
+            device_id=(partner, next_pair * 2 + core),
+            device_id_type=MESH,
+        )
+
+    def grad_onward(other):
+        return pltpu.make_async_remote_copy(
+            src_ref=g_mid.at[other],
+            dst_ref=grad_rows((1 - next_pair) * 2 + core),
+            send_sem=cross_send.at[other],
+            recv_sem=cross_recv.at[core],
+            device_id=(partner, next_pair * 2 + other),
+            device_id_type=MESH,
+        )
+
+    def grad_arrival(other):
+        return pltpu.make_async_remote_copy(
+            src_ref=g_mid.at[other],
+            dst_ref=grad_rows((1 - pair) * 2 + other),
+            send_sem=cross_send.at[other],
+            recv_sem=cross_recv.at[other],
+            device_id=(here, (1 - pair) * 2 + other),
+            device_id_type=MESH,
+        )
+
     def grad_here():
-        return pltpu.make_async_copy(grad_lanes(group), grad_rows(), g_here)
+        return pltpu.make_async_copy(grad_lanes(group), grad_rows(group), g_here)
 
     def out_copy(which, head):
         source, target = (
@@ -185,7 +254,27 @@
             device_id=(here, lax.rem(group + step, groups)),
             device_id_type=MESH,
         )
-    pl.semaphore_wait(barrier, 2 + groups - 1)
+
+    @pl.when(special)
+    def _():
+        for peer in range(groups):
+            pl.semaphore_signal(barrier, inc=1, device_id=(partner, peer), device_id_type=MESH)
+
+    pl.semaphore_wait(barrier, 2 + groups - 1 + jnp.where(special, groups, 0))
+
+    zero_block = jnp.zeros(kv.shape[2:], BF16)
+    for empty, side, slots in ((here == 0, 1, (0, 1)), (here == count - 1, 0, (3, 4))):
+
+        @pl.when(empty)
+        def _():
+            def clear(head, carry):
+                for slot in slots:
+                    kv[head, slot] = zero_block
+                far_in[head, side] = zero_block
+                near_in[head, side] = zero_block
+                return carry
+
+            lax.fori_loop(0, heads, clear, 0)
 
     def send_own(head):
         load(0, head).wait()
@@ -198,13 +287,27 @@
             own_copy(head, side).wait_recv()
             relay_copy(head, side).start()
 
-    for step in range(1, groups):
-        grad_copy(step).start()
-    grad_here().wait()
-    for step in range(1, groups):
-        grad_copy(step).wait_recv()
+    grad_chip().start()
+
+    @pl.when(special)
+    def _():
+        for other in range(2):
+            grad_half(other).start()
+
+    @pl.when(jnp.logical_not(special))
+    def _():
+        for other in range(2):
+            grad_cross(other).start()
+
     send_own(0)
     send_own(1)
+
+    @pl.when(special)
+    def _():
+        for other in range(2):
+            grad_half(other).wait_recv()
+            grad_onward(other).start()
+
 
     zero_tile = jnp.zeros((tile, tile), BF16)
     for t in range(times):
@@ -342,6 +445,13 @@
     def head_step(head, carry):
         load(2, head).wait()
 
+        @pl.when(head == 0)
+        def _():
+            grad_here().wait()
+            grad_chip().wait_recv()
+            for other in range(2):
+                grad_arrival(other).wait_recv()
+
         for side in range(2):
             relay_copy(head, side).wait_recv()
 
@@ -399,8 +509,14 @@
         return carry
 
     lax.fori_loop(0, heads, drain, 0)
-    for step in range(1, groups):
-        grad_copy(step).wait_send()
+    grad_chip().wait_send()
+    for other in range(2):
+        grad_arrival(other).wait_send()
+
+    @pl.when(special)
+    def _():
+        for other in range(2):
+            grad_half(other).wait_send()
 
 
 def forward(times, *refs):
@@ -461,8 +577,13 @@
             pltpu.VMEM((times, WIN + 1, times, tile, tile), BF16),
             dma((heads, 3)),
             dma,
-            dma((groups,)),
-            dma((groups,)),
+            dma,
+            dma,
+            dma((2,)),
+            dma((2,)),
+            dma((2,)),
+            dma((2,)),
+            pltpu.VMEM((2, times, tile // groups, width), BF16),
             dma((heads, 2)),
             dma((heads, 2)),
             dma((heads, 2)),

time: 162 us -> 154 us (0.951)
  the two profiles are of different devices: /device:TPU:1 before, /device:TPU:25 now
where the time goes in v4:
time: 154 us; the launch traced here: 151 us
  Pallas kernels  150 us (97%)
    pallas_call x1, Pallas kernels, shards(): pl.pallas_call(functools.partial(kernel, heads, times, tile, groups), out...  147 us

profile of v4, /device:TPU:25, one launch (start us, length us, event | category | flops | bytes accessed | tf_op | source)
XLA Modules:
  0.0 150.9 jit_solution(15471293597677191566)
XLA Ops:
  0.6 147.5 %band_attention.1 = (bf16[3,256,512]{2,1,0:T(8,128)(2,1)}, bf16[3,256,512]{2,1,0:T(8,128)(2,1)}, bf16[3,256,512]{2,1,0:T(8,128)(2,1)}, bf16[3,256,512]{2,1,0:T(8,128)(2,1)}) custom-call(s32[3,64]{1,0:T(4,128)} %bitcast.18, s32[3,64]{1,0:T(4,128)} %bitcast.19, bf16[3,256,512]{2,1,0:T(8,128)(2,1)} %bitcast.10, bf16[3,256,512]{2,1,0:T(8,128)(2,1)} %bitcast.11, ...), custom_call_target="tpu_custom_call" | custom-call | flops 10871635968 | bytes 6291456 | tf_op jit(solution)/shard_map/band_attention/pallas_call | solution.py:551
  148.1 2.8 %place_results.1 = (bf16[3,256,512]{2,1,0:T(8,128)(2,1)}, bf16[3,256,512]{2,1,0:T(8,128)(2,1)}, bf16[3,256,512]{2,1,0:T(8,128)(2,1)}, bf16[3,256,512]{2,1,0:T(8,128)(2,1)}) custom-call(bf16[3,256,512]{2,1,0:T(8,128)(2,1)} %get-tuple-element.12.refs_0_, bf16[3,256,512]{2,1,0:T(8,128)(2,1)} %get-tuple-element.13.refs_1_, ...), custom_call_target="tpu_custom_call" | custom-call | tf_op jit(solution)/shard_map/place_results/pallas_call | solution.py:605

commit v5 on v4

--- a/solution.py
+++ b/solution.py
@@ -63,10 +63,10 @@
     k_hbm,
     v_hbm,
     g_hbm,
-    att_hbm,
-    dq_hbm,
-    dk_hbm,
-    dv_hbm,
+    att_ref,
+    dq_ref,
+    dk_ref,
+    dv_ref,
     kv,
     far_out,
     far_in,
@@ -76,10 +76,6 @@
     own_sum,
     q_buf,
     g_buf,
-    att_buf,
-    dq_buf,
-    dk_buf,
-    dv_buf,
     k_cur,
     v_cur,
     kt_cur,
@@ -105,7 +101,6 @@
     far_recv,
     near_send,
     near_recv,
-    out_sem,
 ):
     count = lax.axis_size("ctx")
     here = lax.axis_index("ctx")
@@ -162,9 +157,14 @@
             far_out.at[head, side], far_in.at[head, side], far_send, far_recv, head, side
         )
 
-    def near_copy(head, side):
+    def near_copy(head, side, which):
         return remote(
-            near_out.at[head, side], near_in.at[head, side], near_send, near_recv, head, side
+            near_out.at[head, side, which],
+            near_in.at[head, side, which],
+            near_send.at[which],
+            near_recv.at[which],
+            head,
+            side,
         )
 
     def grad_rows(owner):
@@ -228,17 +228,6 @@
     def grad_here():
         return pltpu.make_async_copy(grad_lanes(group), grad_rows(group), g_here)
 
-    def out_copy(which, head):
-        source, target = (
-            (att_buf, att_hbm),
-            (dq_buf, dq_hbm),
-            (dk_buf, dk_hbm),
-            (dv_buf, dv_hbm),
-        )[which]
-        return pltpu.make_async_copy(
-            source.at[head], target.at[:, :, lanes(head)], out_sem.at[which, head]
-        )
-
     for head in range(heads):
         for which in range(3):
             load(which, head).start()
@@ -287,6 +276,7 @@
             own_copy(head, side).wait_recv()
             relay_copy(head, side).start()
 
+    send_own(0)
     grad_chip().start()
 
     @pl.when(special)
@@ -299,7 +289,6 @@
         for other in range(2):
             grad_cross(other).start()
 
-    send_own(0)
     send_own(1)
 
     @pl.when(special)
@@ -362,7 +351,7 @@
 
         att = looped(9, chunks, attend, jnp.zeros((DH, tile), F32))
         rounded = att.astype(BF16).astype(F32)
-        att_buf[head, t] = rounded.T.astype(BF16)
+        att_ref[t, :, lanes(head)] = rounded.T.astype(BF16)
         delta = jnp.sum(g.astype(F32).T * rounded, axis=0, keepdims=True)
 
         def back(i, dq):
@@ -372,7 +361,7 @@
             return dq + dot_nn(kt_cur[rel + s, j], dscores)
 
         dq = looped(9, chunks, back, jnp.zeros((DH, tile), F32))
-        dq_buf[head, t] = (dq * SCALE).T.astype(BF16)
+        dq_ref[t, :, lanes(head)] = (dq * SCALE).T.astype(BF16)
 
     def key_side(head):
         rels = [jnp.clip(start_ref[t, here] - here + OWN, 0, OWN) for t in range(times)]
@@ -423,24 +412,22 @@
                     return carry
 
                 lax.fori_loop(0, times, one, 0)
-            near_copy(head, side).start()
+                near_copy(head, side, which).start()
 
     def finish(head):
-        for side in range(2):
-            near_copy(head, side).wait_recv()
-
-        def one(j, carry):
-            for which, out in enumerate((dk_buf, dv_buf)):
-                out[head, j] = (
+        for which, out in enumerate((dk_ref, dv_ref)):
+            for side in range(2):
+                near_copy(head, side, which).wait_recv()
+
+            def one(j, carry, which=which, out=out):
+                out[j, :, lanes(head)] = (
                     own_sum[head, which, j]
                     + near_in[head, 0, which, j].astype(F32)
                     + near_in[head, 1, which, j].astype(F32)
                 ).astype(BF16)
-            return carry
-
-        lax.fori_loop(0, times, one, 0)
-        out_copy(2, head).start()
-        out_copy(3, head).start()
+                return carry
+
+            lax.fori_loop(0, times, one, 0)
 
     def head_step(head, carry):
         load(2, head).wait()
@@ -469,43 +456,41 @@
 
         def visit(t, inner):
             tile_step(head, t)
+
+            @pl.when((head == 0) & (t == 1))
+            def _():
+                send_relay(2)
+
+            @pl.when((head == 1) & (t == 1))
+            def _():
+                send_relay(3)
+                for side in range(2):
+                    far_copy(0, side).start()
+
             return inner
 
         lax.fori_loop(0, times, visit, 0)
-        out_copy(0, head).start()
-        out_copy(1, head).start()
         key_side(head)
-
-        @pl.when(head == 0)
-        def _():
-            for later in range(2, heads):
-                send_relay(later)
-            for side in range(2):
-                far_copy(head, side).start()
-
-        @pl.when(head > 0)
-        def _():
-            send_near(head - 1)
 
         @pl.when(head > 1)
         def _():
-            finish(head - 2)
+            send_near(head - 2)
 
         return carry
 
     lax.fori_loop(0, heads, head_step, 0)
-    send_near(heads - 1)
-    finish(heads - 2)
-    finish(heads - 1)
+    for head in range(heads - 2, heads):
+        send_near(head)
+    for head in range(heads):
+        finish(head)
 
     def drain(head, carry):
         for side in range(2):
             own_copy(head, side).wait_send()
             relay_copy(head, side).wait_send()
             far_copy(head, side).wait_send()
-            near_copy(head, side).wait_send()
-        for which in range(4):
-            out_copy(which, head).wait()
+            for which in range(2):
+                near_copy(head, side, which).wait_send()
         return carry
 
     lax.fori_loop(0, heads, drain, 0)
@@ -520,21 +505,15 @@
 
 
 def forward(times, *refs):
-    sources, targets = refs[:4], refs[4:8]
-    held, in_sem, out_sem = refs[8:]
-    pieces = [(i, t) for t in range(times) for i in range(4)]
-    inward = [
-        pltpu.make_async_copy(sources[i].at[t], held.at[i, t], in_sem.at[i, t]) for i, t in pieces
+    sources, targets, sems = refs[:4], refs[4:8], refs[8]
+    copies = [
+        pltpu.make_async_copy(sources[i].at[t], targets[i].at[t], sems.at[i, t])
+        for t in range(times)
+        for i in range(4)
     ]
-    outward = [
-        pltpu.make_async_copy(held.at[i, t], targets[i].at[t], out_sem.at[i, t]) for i, t in pieces
-    ]
-    for copy in inward:
+    for copy in copies:
         copy.start()
-    for first, second in zip(inward, outward):
-        first.wait()
-        second.start()
-    for copy in outward:
+    for copy in copies:
         copy.wait()
 
 
@@ -545,14 +524,15 @@
     block = (times, tile, DH)
     dma = pltpu.SemaphoreType.DMA
     any_spec = pl.BlockSpec(memory_space=pl.ANY)
+    vmem_spec = pl.BlockSpec(memory_space=pltpu.VMEM)
     smem_spec = pl.BlockSpec(memory_space=pltpu.SMEM)
     out = jax.ShapeDtypeStruct((times, tile, width), BF16)
     pairs = times * heads * 6 * tile * WIN * times * tile * DH * 2
     results = pl.pallas_call(
         functools.partial(kernel, heads, times, tile, groups),
-        out_shape=(out,) * 4,
+        out_shape=(pltpu.VMEM(out.shape, BF16),) * 4,
         in_specs=[smem_spec, smem_spec] + [any_spec] * 4,
-        out_specs=(any_spec,) * 4,
+        out_specs=(vmem_spec,) * 4,
         scratch_shapes=[
             pltpu.VMEM((heads, SLOTS, 2) + block, BF16),
             pltpu.VMEM((heads, 2, 2) + block, BF16),
@@ -563,10 +543,6 @@
             pltpu.VMEM((heads, 2) + block, F32),
             pltpu.VMEM((heads,) + block, BF16),
             pltpu.VMEM((times, tile, width), BF16),
-            pltpu.VMEM((heads,) + block, BF16),
-            pltpu.VMEM((heads,) + block, BF16),
-            pltpu.VMEM((heads,) + block, BF16),
-            pltpu.VMEM((heads,) + block, BF16),
             pltpu.VMEM((SLOTS, times, tile, DH), BF16),
             pltpu.VMEM((SLOTS, times, tile, DH), BF16),
             pltpu.VMEM((SLOTS, times, DH, tile), BF16),
@@ -590,12 +566,11 @@
             dma((heads, 2)),
             dma((heads, 2)),
             dma((heads, 2)),
-            dma((heads, 2)),
-            dma((heads, 2)),
-            dma((4, heads)),
+            dma((2, heads, 2)),
+            dma((2, heads, 2)),
         ],
         compiler_params=pltpu.CompilerParams(
-            collective_id=0, has_side_effects=True, vmem_limit_bytes=60 * 1024 * 1024
+            collective_id=0, has_side_effects=True, vmem_limit_bytes=54 * 1024 * 1024
         ),
         cost_estimate=pl.CostEstimate(
             flops=pairs, bytes_accessed=8 * times * tile * width * 2, transcendentals=0
@@ -605,13 +580,10 @@
     results = pl.pallas_call(
         functools.partial(forward, times),
         out_shape=(out,) * 4,
-        in_specs=[any_spec] * 4,
+        in_specs=[vmem_spec] * 4,
         out_specs=(any_spec,) * 4,
-        scratch_shapes=[
-            pltpu.VMEM((4, times, tile, width), BF16),
-            dma((4, times)),
-            dma((4, times)),
-        ],
+        scratch_shapes=[dma((4, times))],
+        compiler_params=pltpu.CompilerParams(vmem_limit_bytes=4 * 1024 * 1024),
         name="place_results",
     )(*results)
     return tuple(result[None] for result in results)

time: 154 us -> 152 us (0.987)
  Pallas kernels: 150 us -> 148 us
where the time goes in v5:
time: 152 us; the launch traced here: 149 us
  Pallas kernels  148 us (97%)
    pallas_call x1, Pallas kernels, shards(): pl.pallas_call(functools.partial(kernel, heads, times, tile, groups), out...  147 us

profile of v5, /device:TPU:25, one launch (start us, length us, event | category | flops | bytes accessed | tf_op | source)
XLA Modules:
  0.0 149.1 jit_solution(890648112103774148)
XLA Ops:
  0.6 146.7 %band_attention.1 = (bf16[3,256,512]{2,1,0:T(8,128)(2,1)S(1)}, bf16[3,256,512]{2,1,0:T(8,128)(2,1)S(1)}, bf16[3,256,512]{2,1,0:T(8,128)(2,1)S(1)}, bf16[3,256,512]{2,1,0:T(8,128)(2,1)S(1)}) custom-call(s32[3,64]{1,0:T(4,128)} %bitcast.18, s32[3,64]{1,0:T(4,128)} %bitcast.19, bf16[3,256,512]{2,1,0:T(8,128)(2,1)} %bitcast.10, bf16[3,256,512]{2,1,0:T(8,128)(2,1)} %bitcast.11, ...), custom_call_target="tpu_custom_call" | custom-call | flops 10871635968 | bytes 6291456 | tf_op jit(solution)/shard_map/band_attention/pallas_call | solution.py:531
  147.3 1.8 %place_results.1 = (bf16[3,256,512]{2,1,0:T(8,128)(2,1)}, bf16[3,256,512]{2,1,0:T(8,128)(2,1)}, bf16[3,256,512]{2,1,0:T(8,128)(2,1)}, bf16[3,256,512]{2,1,0:T(8,128)(2,1)}) custom-call(bf16[3,256,512]{2,1,0:T(8,128)(2,1)S(1)} %get-tuple-element.12.refs_0_, bf16[3,256,512]{2,1,0:T(8,128)(2,1)S(1)} %get-tuple-element.13.refs_1_, ...), custom_call_target="tpu_custom_call" | custom-call | tf_op jit(solution)/shard_map/place_results/pallas_call | solution.py:580

commit v6 on v5

--- a/solution.py
+++ b/solution.py
@@ -228,10 +228,6 @@
     def grad_here():
         return pltpu.make_async_copy(grad_lanes(group), grad_rows(group), g_here)
 
-    for head in range(heads):
-        for which in range(3):
-            load(which, head).start()
-    grad_here().start()
 
     barrier = pltpu.get_barrier_semaphore()
     for neighbour in toward:
@@ -249,7 +245,42 @@
         for peer in range(groups):
             pl.semaphore_signal(barrier, inc=1, device_id=(partner, peer), device_id_type=MESH)
 
+    for which in range(2):
+        load(which, 0).start()
     pl.semaphore_wait(barrier, 2 + groups - 1 + jnp.where(special, groups, 0))
+
+    def send_own(head):
+        load(0, head).wait()
+        load(1, head).wait()
+        for side in range(2):
+            own_copy(head, side).start()
+
+    def send_relay(head):
+        for side in (1, 0):
+            own_copy(head, side).wait_recv()
+            relay_copy(head, side).start()
+
+    send_own(0)
+    for which in range(2):
+        load(which, 1).start()
+    grad_chip().start()
+
+    @pl.when(special)
+    def _():
+        for other in range(2):
+            grad_half(other).start()
+
+    @pl.when(jnp.logical_not(special))
+    def _():
+        for other in range(2):
+            grad_cross(other).start()
+
+    send_own(1)
+    for head in range(heads):
+        for which in range(3):
+            if which == 2 or head > 1:
+                load(which, head).start()
+    grad_here().start()
 
     zero_block = jnp.zeros(kv.shape[2:], BF16)
     for empty, side, slots in ((here == 0, 1, (0, 1)), (here == count - 1, 0, (3, 4))):
@@ -265,38 +296,11 @@
 
             lax.fori_loop(0, heads, clear, 0)
 
-    def send_own(head):
-        load(0, head).wait()
-        load(1, head).wait()
-        for side in range(2):
-            own_copy(head, side).start()
-
-    def send_relay(head):
-        for side in (1, 0):
-            own_copy(head, side).wait_recv()
-            relay_copy(head, side).start()
-
-    send_own(0)
-    grad_chip().start()
-
-    @pl.when(special)
-    def _():
-        for other in range(2):
-            grad_half(other).start()
-
-    @pl.when(jnp.logical_not(special))
-    def _():
-        for other in range(2):
-            grad_cross(other).start()
-
-    send_own(1)
-
     @pl.when(special)
     def _():
         for other in range(2):
             grad_half(other).wait_recv()
             grad_onward(other).start()
-
 
     zero_tile = jnp.zeros((tile, tile), BF16)
     for t in range(times):
@@ -481,7 +485,7 @@
     lax.fori_loop(0, heads, head_step, 0)
     for head in range(heads - 2, heads):
         send_near(head)
-    for head in range(heads):
+    for head in range(heads - 1):
         finish(head)
 
     def drain(head, carry):
@@ -489,11 +493,16 @@
             own_copy(head, side).wait_send()
             relay_copy(head, side).wait_send()
             far_copy(head, side).wait_send()
+        return carry
+
+    def drain_near(head, carry):
+        for side in range(2):
             for which in range(2):
                 near_copy(head, side, which).wait_send()
         return carry
 
     lax.fori_loop(0, heads, drain, 0)
+    lax.fori_loop(0, heads - 1, drain_near, 0)
     grad_chip().wait_send()
     for other in range(2):
         grad_arrival(other).wait_send()
@@ -502,6 +511,9 @@
     def _():
         for other in range(2):
             grad_half(other).wait_send()
+
+    finish(heads - 1)
+    drain_near(heads - 1, 0)
 
 
 def forward(times, *refs):

time: 152 us -> 152 us (level)
  no operation moved by 1% of the time
where the time goes in v6:
time: 152 us; the launch traced here: 149 us
  Pallas kernels  148 us (97%)
    pallas_call x1, Pallas kernels, shards(): pl.pallas_call(functools.partial(kernel, heads, times, tile, groups), out...  147 us

profile of v6, /device:TPU:25, one launch (start us, length us, event | category | flops | bytes accessed | tf_op | source)
XLA Modules:
  0.0 149.0 jit_solution(2612709783113243171)
XLA Ops:
  0.6 146.6 %band_attention.1 = (bf16[3,256,512]{2,1,0:T(8,128)(2,1)S(1)}, bf16[3,256,512]{2,1,0:T(8,128)(2,1)S(1)}, bf16[3,256,512]{2,1,0:T(8,128)(2,1)S(1)}, bf16[3,256,512]{2,1,0:T(8,128)(2,1)S(1)}) custom-call(s32[3,64]{1,0:T(4,128)} %bitcast.18, s32[3,64]{1,0:T(4,128)} %bitcast.19, bf16[3,256,512]{2,1,0:T(8,128)(2,1)} %bitcast.10, bf16[3,256,512]{2,1,0:T(8,128)(2,1)} %bitcast.11, ...), custom_call_target="tpu_custom_call" | custom-call | flops 10871635968 | bytes 6291456 | tf_op jit(solution)/shard_map/band_attention/pallas_call | solution.py:543
  147.2 1.8 %place_results.1 = (bf16[3,256,512]{2,1,0:T(8,128)(2,1)}, bf16[3,256,512]{2,1,0:T(8,128)(2,1)}, bf16[3,256,512]{2,1,0:T(8,128)(2,1)}, bf16[3,256,512]{2,1,0:T(8,128)(2,1)}) custom-call(bf16[3,256,512]{2,1,0:T(8,128)(2,1)S(1)} %get-tuple-element.12.refs_0_, bf16[3,256,512]{2,1,0:T(8,128)(2,1)S(1)} %get-tuple-element.13.refs_1_, ...), custom_call_target="tpu_custom_call" | custom-call | tf_op jit(solution)/shard_map/place_results/pallas_call | solution.py:592

commit v7 on v6

--- a/solution.py
+++ b/solution.py
@@ -516,12 +516,10 @@
     drain_near(heads - 1, 0)
 
 
-def forward(times, *refs):
+def forward(*refs):
     sources, targets, sems = refs[:4], refs[4:8], refs[8]
     copies = [
-        pltpu.make_async_copy(sources[i].at[t], targets[i].at[t], sems.at[i, t])
-        for t in range(times)
-        for i in range(4)
+        pltpu.make_async_copy(sources[i], targets[i], sems.at[i]) for i in range(4)
     ]
     for copy in copies:
         copy.start()
@@ -590,11 +588,11 @@
         name="band_attention",
     )(window_start.T, key_counts.T, queries[0], keys[0], values[0], grad_out[0])
     results = pl.pallas_call(
-        functools.partial(forward, times),
+        forward,
         out_shape=(out,) * 4,
         in_specs=[vmem_spec] * 4,
         out_specs=(any_spec,) * 4,
-        scratch_shapes=[dma((4, times))],
+        scratch_shapes=[dma((4,))],
         compiler_params=pltpu.CompilerParams(vmem_limit_bytes=4 * 1024 * 1024),
         name="place_results",
     )(*results)

time: 152 us -> 152 us (level)
  no operation moved by 1% of the time
where the time goes in v7:
time: 152 us; the launch traced here: 149 us
  Pallas kernels  148 us (97%)
    pallas_call x1, Pallas kernels, shards(): pl.pallas_call(functools.partial(kernel, heads, times, tile, groups), out...  147 us

profile of v7, /device:TPU:25, one launch (start us, length us, event | category | flops | bytes accessed | tf_op | source)
XLA Modules:
  0.0 148.9 jit_solution(8967967893719160357)
XLA Ops:
  0.6 146.6 %band_attention.1 = (bf16[3,256,512]{2,1,0:T(8,128)(2,1)S(1)}, bf16[3,256,512]{2,1,0:T(8,128)(2,1)S(1)}, bf16[3,256,512]{2,1,0:T(8,128)(2,1)S(1)}, bf16[3,256,512]{2,1,0:T(8,128)(2,1)S(1)}) custom-call(s32[3,64]{1,0:T(4,128)} %bitcast.18, s32[3,64]{1,0:T(4,128)} %bitcast.19, bf16[3,256,512]{2,1,0:T(8,128)(2,1)} %bitcast.10, bf16[3,256,512]{2,1,0:T(8,128)(2,1)} %bitcast.11, ...), custom_call_target="tpu_custom_call" | custom-call | flops 10871635968 | bytes 6291456 | tf_op jit(solution)/shard_map/band_attention/pallas_call | solution.py:541
  147.2 1.7 %place_results.1 = (bf16[3,256,512]{2,1,0:T(8,128)(2,1)}, bf16[3,256,512]{2,1,0:T(8,128)(2,1)}, bf16[3,256,512]{2,1,0:T(8,128)(2,1)}, bf16[3,256,512]{2,1,0:T(8,128)(2,1)}) custom-call(bf16[3,256,512]{2,1,0:T(8,128)(2,1)S(1)} %get-tuple-element.12.refs_0_, bf16[3,256,512]{2,1,0:T(8,128)(2,1)S(1)} %get-tuple-element.13.refs_1_, ...), custom_call_target="tpu_custom_call" | custom-call | tf_op jit(solution)/shard_map/place_results/pallas_call | solution.py:590
